TPU v7x, 32 devices: a whole 2x2x4 slice. The times are simulated.
32 devices in a mesh: dp: 8 (over z, x), fsdp: 4 (over y, core).
Axes of the slice: x: 2, y: 2, z: 4, core: 2. Of those that a mesh axis runs over, the one named last changes fastest.
Arguments:
- tokens: bfloat16 [16384, 1024], P(('dp', 'fsdp')), may hold values from -6 to 6
- cotangent: bfloat16 [16384, 1024], P(('dp', 'fsdp')), may hold values from -6 to 6
- prot_lens: int32 [32, 8], P(('dp', 'fsdp')), may hold values from 0 to 512, as said below
- clus_start: int32 [32, 8], P(('dp', 'fsdp')), may hold values 0 or 1
- norm_gain: bfloat16 [1024], P('fsdp'), may hold values from 0.5 to 1.5
- in_w: bfloat16 [1024, 4096], P('fsdp'), may hold values from -0.1875 to 0.1875
- conv_w: bfloat16 [4, 2048], P(None, 'fsdp'), may hold values from -3 to 3
- conv_b: bfloat16 [2048], P('fsdp'), may hold values from -3 to 3
- xproj_w: bfloat16 [2048, 96], P('fsdp'), may hold values from -0.125 to 0.125
- dtproj_w: bfloat16 [64, 2048], P(None, 'fsdp'), may hold values from -0.75 to 0.75
- dt_bias: bfloat16 [2048], P('fsdp'), may hold values from -6.875 to -2.296875
- a_log: bfloat16 [16, 2048], P(None, 'fsdp'), may hold values from 0 to 2.765625
- d_skip: bfloat16 [2048], P('fsdp'), may hold values from 0.5 to 1.5
- out_w: bfloat16 [2048, 1024], P('fsdp'), may hold values from -0.25 to 0.25
Outputs:
- mixed: bfloat16 [16384, 1024], P(('dp', 'fsdp'))
- token_grad: float32 [16384, 1024], P(('dp', 'fsdp'))
- gain_grad: float32 [1024], P('fsdp')
- in_grad: float32 [1024, 4096], P('fsdp')
- conv_grad: float32 [4, 2048], P(None, 'fsdp')
- conv_bias_grad: float32 [2048], P('fsdp')
- xproj_grad: float32 [2048, 96], P('fsdp')
- dtproj_grad: float32 [64, 2048], P(None, 'fsdp')
- dt_bias_grad: float32 [2048], P('fsdp')
- a_log_grad: float32 [16, 2048], P(None, 'fsdp')
- skip_grad: float32 [2048], P('fsdp')
- out_grad: float32 [2048, 1024], P('fsdp')
Inputs may be any that keep to these rules, and one draw needn't show every extreme that they name: `prot_lens`: each row lists the lengths of the proteins in one buffer, in order, then zeros; a protein has 50 to 512 residues, a row sums to at most 512, and some buffer holds a single protein of 512 residues. `clus_start`: row r marks which protein slots of buffer r begin a new cluster; a cluster runs on over the following proteins of the buffer until the next mark.
All inputs are finite; a program needn't handle non-finite values. No bound on the sum of `clus_start` on one device may be relied on, other than what follows from the above.
Results may differ from a plain program's by a relative error of at most 0.011.
Values may be sent and summed in bfloat16 or wider, within the bound.
A program may use at most 320 MiB of HBM per device.

v0:
```python
import functools

import jax
import jax.numpy as jnp
from jax import lax
from jax.experimental import pallas as pl
from jax.experimental.pallas import tpu as pltpu
from jax.sharding import PartitionSpec as P

QLEN = 16
LANES = 128
WIDE = 256
NEVER = 1e30
LOG2E = 1.4426950408889634
FORWARD_STEPS = (0, 2, 3, 4, 5, 6)
BACKWARD_STEPS = (0, 3, 7, 10, 12, 14, 15)


EPSILON = 1e-05


def shifted_down(values, offset):
    padding = jnp.zeros((offset,) + values.shape[1:], values.dtype)
    return jnp.concatenate([padding, values[:-offset]], axis=0)


def protein_masks(lens_row, start_row, length, taps):
    protein_ends = jnp.cumsum(lens_row)
    protein_begins = protein_ends - lens_row
    flagged = (start_row > 0) & (lens_row > 0)
    position = jnp.arange(length, dtype=jnp.int32)
    cluster = jnp.sum(
        ((position[:, None] >= protein_begins[None, :]) & flagged[None, :]).astype(jnp.int32),
        axis=1,
    )
    live_mask = (position < protein_ends[-1]).astype(jnp.float32)
    same_masks = []
    for offset in range(1, taps):
        matching = (position >= offset) & (cluster == shifted_down(cluster, offset))
        same_masks.append(matching.astype(jnp.float32))
    return (live_mask, same_masks)


def rows_product(left, right):
    return lax.dot_general(
        left, right, (((0,), (0,)), ((), ())), preferred_element_type=jnp.float32
    )


def transposed_product(left, weight):
    return lax.dot_general(
        left, weight, (((1,), (1,)), ((), ())), preferred_element_type=jnp.float32
    )


MESH = pl.DeviceIdType.MESH
GROUP = 8


def own_bits():
    d, f = lax.axis_index("dp"), lax.axis_index("fsdp")
    inside = lax.rem(d, GROUP)
    return {
        "pair": f // 2,
        "core": lax.rem(f, 2),
        "high": inside // 4,
        "low": lax.rem(inside // 2, 2),
        "bit": lax.rem(inside, 2),
    }


def across(own, dim):
    d, f = lax.axis_index("dp"), lax.axis_index("fsdp")
    step = {"pair": 2, "core": 1, "high": 4, "low": 2, "bit": 1}[dim]
    flip = step * (1 - 2 * own[dim])
    return (d, f + flip) if dim in ("pair", "core") else (d + flip, f)


def greet(own, dims):
    barrier = pltpu.get_barrier_semaphore()
    for dim in dims:
        pl.semaphore_signal(barrier, inc=1, device_id=across(own, dim), device_id_type=MESH)
    pl.semaphore_wait(barrier, len(dims))


class Link:
    def __init__(self, own):
        self.own = own
        self.sent = []

    def copy(self, src, dst, sems, dim):
        return pltpu.make_async_remote_copy(
            src_ref=src,
            dst_ref=dst,
            send_sem=sems[0],
            recv_sem=sems[1],
            device_id=across(self.own, dim),
            device_id_type=MESH,
        )

    def send(self, described):
        self.copy(*described()).start()
        self.sent.append(described)

    def receive(self, ref, sems, dim):
        self.copy(ref, ref, sems, dim).wait_recv()

    def finish(self):
        for described in self.sent:
            self.copy(*described()).wait_send()


class Gather:
    def __init__(self, shards, outs, scratch):
        self.shards, self.outs = shards, outs
        self.count = len(shards)
        self.stage = scratch[: self.count]
        self.load_sem, self.core_sem, self.hop_sem, self.whole_sem = scratch[self.count :]
        self.own = own_bits()
        self.link = Link(self.own)
        pair, core = self.own["pair"], self.own["core"]
        self.mine = 2 * pair + core
        self.theirs = 2 * (1 - pair) + core
        self.sibling = 2 * pair + 1 - core
        self.beyond = 2 * (1 - pair) + 1 - core
        bit, low = self.own["bit"], self.own["low"]
        self.kinds = ((bit, low), (1 - bit, low), (bit, 1 - low), (1 - bit, 1 - low))
        self.stages = [self.begin, *(functools.partial(self.from_pair, half) for half in range(2))]
        self.stages += [*(functools.partial(self.from_near, half) for half in range(2)), self.from_far, self.end]

    def eighth(self, a, kind, half):
        rows = self.shards[a].shape[0] // 8
        bit, low = self.kinds[kind]
        return pl.ds(pl.multiple_of((2 * (bit + 2 * low) + half) * rows, rows), rows)

    def hop(self, a, kind, half):
        return self.hop_sem.at[0, a, kind, half], self.hop_sem.at[1, a, kind, half]

    def to_core(self, a, kind, half):
        return self.core_sem.at[0, a, kind, half], self.core_sem.at[1, a, kind, half]

    def whole(self, a):
        return self.whole_sem.at[0, a], self.whole_sem.at[1, a]

    def load(self, a):
        return pltpu.make_async_copy(self.shards[a], self.stage[a], self.load_sem.at[a])

    def store(self, a):
        return pltpu.make_async_copy(self.stage[a], self.outs[a].at[self.mine], self.load_sem.at[a])

    def begin(self):
        greet(self.own, ("core", "pair", "bit", "low"))
        for half in range(2):
            for a in range(self.count):
                self.link.send(functools.partial(self.to_pair, a, half))
        for a in range(self.count):
            self.load(a).start()
            self.link.send(functools.partial(self.own_to_core, a))

    def to_pair(self, a, half):
        rows = self.eighth(a, 0, half)
        return self.shards[a].at[rows], self.outs[a].at[self.mine, rows], self.hop(a, 0, half), "pair"

    def own_to_core(self, a):
        return self.shards[a], self.outs[a].at[self.mine], self.whole(a), "core"

    def came(self, a, kind, half):
        return self.outs[a].at[self.theirs, self.eighth(a, kind, half)]

    def onward(self, a, kind, half, new_kind, dim):
        ref = self.came(a, kind, half)
        return ref, ref, self.to_core(a, kind, half) if dim == "core" else self.hop(a, new_kind, half), dim

    def pass_on(self, a, kind, half, new_kind, dim):
        self.link.send(functools.partial(self.onward, a, kind, half, new_kind, dim))

    def arrive(self, a, kind, half, dim):
        self.link.receive(self.came(a, kind, half), self.hop(a, kind, half), dim)
        self.pass_on(a, kind, half, kind, "core")

    def from_pair(self, half):
        for a in range(self.count):
            self.arrive(a, 0, half, "pair")
            self.pass_on(a, 0, half, 1, "bit")
            self.pass_on(a, 0, half, 2, "low")
        if half == 1:
            for a in range(self.count):
                self.load(a).wait()
                self.store(a).start()

    def from_near(self, half):
        for a in range(self.count):
            self.arrive(a, 1, half, "bit")
            if half == 0:
                self.pass_on(a, 1, 0, 3, "low")
            self.arrive(a, 2, half, "low")
            if half == 1:
                self.pass_on(a, 2, 1, 3, "bit")

    def from_far(self):
        for a in range(self.count):
            self.arrive(a, 3, 0, "low")
            self.arrive(a, 3, 1, "bit")

    def end(self):
        for a in range(self.count):
            self.link.receive(self.outs[a].at[self.sibling], self.whole(a), "core")
            for kind in range(4):
                for half in range(2):
                    ref = self.outs[a].at[self.beyond, self.eighth(a, kind, half)]
                    self.link.receive(ref, self.to_core(a, kind, half), "core")
            self.store(a).wait()
        self.link.finish()

    @staticmethod
    def scratch(shards):
        count = len(shards)
        dma = pltpu.SemaphoreType.DMA
        staged = [pltpu.VMEM(s.shape, s.dtype) for s in shards]
        return staged + [dma((count,)), dma((2, count, 4, 2)), dma((2, count, 4, 2)), dma((2, count))]


def gather_kernel(count, *refs):
    for stage in Gather(refs[:count], refs[count : 2 * count], refs[2 * count :]).stages:
        stage()


def gathered_shape(shard):
    return jax.ShapeDtypeStruct((4,) + shard.shape, shard.dtype)


def gather_weights(shards, collective_id):
    count = len(shards)
    return pl.pallas_call(
        functools.partial(gather_kernel, count),
        out_shape=[gathered_shape(s) for s in shards],
        in_specs=[pl.BlockSpec(memory_space=pl.ANY)] * count,
        out_specs=[pl.BlockSpec(memory_space=pl.ANY)] * count,
        scratch_shapes=Gather.scratch(shards),
        compiler_params=pltpu.CompilerParams(
            collective_id=collective_id, has_side_effects=True, vmem_limit_bytes=32 << 20
        ),
        name="gather_weights",
    )(*shards)


def run_stages(stages, at_steps):
    for step in sorted(set(at_steps)):

        @pl.when(pl.program_id(0) == step)
        def _():
            for stage, at in zip(stages, at_steps):
                if at == step:
                    stage()


DIMS = ("pair", "high", "low", "bit")
HALVE = (("pair", "bit", "low", "high"), ("bit", "low", "pair", "high"), ("low", "pair", "bit", "high"))
SPREAD = (("high", "bit", "low"), ("high", "low", "bit"), ("high", "bit", "low"))
EVERY = slice(None)


def each_block(free, body):
    if not free:
        body(())
        return

    def step(i, carried):
        body(tuple(lax.rem(i // 2 ** (free - 1 - n), 2) for n in range(free)))
        return carried

    lax.fori_loop(0, 2**free, step, 0)


def cut_parts(shape):
    axis, tile = (1, 128) if shape[1] >= 512 else (0, 16)
    tiles = shape[axis] // tile
    sizes = [(tiles + 2 - k) // 3 * tile for k in range(3)]
    return [(axis, sum(sizes[:k]), sizes[k]) for k in range(3)]


class Reduction:
    def __init__(self, grads, outs, scratch):
        count = len(grads)
        self.grads, self.outs = grads, outs
        self.accs, self.cores, self.fulls = (scratch[i * count : (i + 1) * count] for i in range(3))
        rest = scratch[3 * count :]
        self.arrived = [[[rest[(s * count + a) * 3 + k] for k in range(3)] for a in range(count)] for s in range(4)]
        self.load_sem, self.core_sem, self.half_sem, self.full_sem, self.out_sem = rest[12 * count :]
        self.parts = [cut_parts(g.shape[4:]) for g in grads]
        self.jobs = [(k, a) for k in range(3) for a in range(count)]
        self.own = own_bits()
        self.link = Link(self.own)
        self.stages = [self.begin, self.join, *(functools.partial(self.halved, s) for s in range(4))]
        self.stages += [*(functools.partial(self.spread, s) for s in range(3)), self.end]

    def part(self, k, a):
        axis, start, size = self.parts[a][k]
        return (pl.ds(start, size), EVERY) if axis == 0 else (EVERY, pl.ds(start, size))

    def region(self, chosen, dims, k, a):
        return tuple(chosen.get(d, EVERY) for d in dims) + self.part(k, a)

    def loading(self, k, a, y):
        at = self.region({"pair": y}, DIMS, k, a)
        kept = (2 * y + self.own["core"],) + at[1:]
        return pltpu.make_async_copy(self.grads[a].at[kept], self.accs[a].at[at], self.load_sem.at[a, k, y])

    def begin(self):
        greet(self.own, ("core", "pair", "bit", "low", "high"))
        for k, a in self.jobs:
            for y in range(2):
                self.link.send(functools.partial(self.given, k, a, y))
                self.loading(k, a, y).start()

    def given(self, k, a, y):
        at = self.region({"pair": y}, DIMS, k, a)
        other = (2 * y + 1 - self.own["core"],) + at[1:]
        sems = (self.core_sem.at[0, a, k, y], self.core_sem.at[1, a, k, y])
        return self.grads[a].at[other], self.cores[a].at[at], sems, "core"

    def half(self, k, a, step):
        dim = HALVE[k][step]
        chosen = {d: self.own[d] for d in HALVE[k][:step]}
        chosen[dim] = 1 - self.own[dim]
        sems = (self.half_sem.at[0, a, k, step], self.half_sem.at[1, a, k, step])
        return self.accs[a].at[self.region(chosen, DIMS, k, a)], self.arrived[step][a][k], sems, dim

    def halve(self, k, a, step):
        self.link.send(functools.partial(self.half, k, a, step))

    def join(self):
        for k, a in self.jobs:
            for y in range(2):
                self.loading(k, a, y).wait()
                sems = (self.core_sem.at[0, a, k, y], self.core_sem.at[1, a, k, y])
                self.link.receive(self.cores[a].at[self.region({"pair": y}, DIMS, k, a)], sems, "core")

            def add(lead):
                at = lead + self.part(k, a)
                self.accs[a][at] = self.accs[a][at] + self.cores[a][at]

            each_block(4, add)
            self.halve(k, a, 0)

    def halved(self, step):
        for k, a in self.jobs:
            sems = (self.half_sem.at[0, a, k, step], self.half_sem.at[1, a, k, step])
            self.link.receive(self.arrived[step][a][k], sems, HALVE[k][step])
            chosen = {d: self.own[d] for d in HALVE[k][: step + 1]}
            free = [d for d in DIMS if d not in chosen]

            def add(lead):
                at = tuple(chosen[d] if d in chosen else lead[free.index(d)] for d in DIMS) + self.part(k, a)
                total = self.accs[a][at] + self.arrived[step][a][k][lead + (EVERY, EVERY)]
                if step < 3:
                    self.accs[a][at] = total
                else:
                    self.fulls[a][at[1:]] = total

            each_block(len(free), add)
            if step < 3:
                self.halve(k, a, step + 1)
            else:
                self.pass_on(k, a, 0)

    def held(self, k, a, step):
        chosen = {d: self.own[d] for d in SPREAD[k][step:]}
        here = self.fulls[a].at[self.region(chosen, DIMS[1:], k, a)]
        return here, here, (self.full_sem.at[0, a, k, step], self.full_sem.at[1, a, k, step]), SPREAD[k][step]

    def pass_on(self, k, a, step):
        self.link.send(functools.partial(self.held, k, a, step))

    def spread(self, step):
        for k, a in self.jobs:
            chosen = {d: self.own[d] for d in SPREAD[k][step:]}
            dim = SPREAD[k][step]
            chosen[dim] = 1 - self.own[dim]
            there = self.fulls[a].at[self.region(chosen, DIMS[1:], k, a)]
            self.link.receive(there, (self.full_sem.at[0, a, k, step], self.full_sem.at[1, a, k, step]), dim)
            if step < 2:
                self.pass_on(k, a, step + 1)

    def end(self):
        stores = [
            pltpu.make_async_copy(self.fulls[a], self.outs[a], self.out_sem.at[a]) for a in range(len(self.outs))
        ]
        for copy in stores:
            copy.start()
        for copy in stores:
            copy.wait()
        self.link.finish()

    @staticmethod
    def scratch(grads):
        count = len(grads)
        dma = pltpu.SemaphoreType.DMA
        low = jnp.bfloat16
        shapes = [pltpu.VMEM((2, 2, 2, 2) + g.shape[4:], low) for g in grads] * 2
        shapes += [pltpu.VMEM((2, 2, 2) + g.shape[4:], low) for g in grads]
        for step in range(4):
            for g in grads:
                for axis, _, size in cut_parts(g.shape[4:]):
                    block = (size, g.shape[5]) if axis == 0 else (g.shape[4], size)
                    shapes.append(pltpu.VMEM((2,) * (3 - step) + block, low))
        return shapes + [
            dma((count, 3, 2)),
            dma((2, count, 3, 2)),
            dma((2, count, 3, 4)),
            dma((2, count, 3, 3)),
            dma((count,)),
        ]


def reduce_kernel(count, *refs):
    for stage in Reduction(refs[:count], refs[count : 2 * count], refs[2 * count :]).stages:
        stage()


def reduce_gradients(grads, collective_id):
    count = len(grads)
    return pl.pallas_call(
        functools.partial(reduce_kernel, count),
        out_shape=[jax.ShapeDtypeStruct(g.shape[1:], g.dtype) for g in grads],
        in_specs=[pl.BlockSpec(memory_space=pl.ANY)] * count,
        out_specs=[pl.BlockSpec(memory_space=pl.ANY)] * count,
        scratch_shapes=Reduction.scratch(grads),
        compiler_params=pltpu.CompilerParams(
            collective_id=collective_id, has_side_effects=True, vmem_limit_bytes=56 << 20
        ),
        name="reduce_gradients",
    )(*grads)


def block_rows(values, row, rows):
    return values[row : row + 1, :]


def lane_index(shape):
    return lax.broadcasted_iota(jnp.int32, shape, 1)


def dot(left, right):
    return jnp.dot(left, right, preferred_element_type=jnp.float32)


def smooth(values):
    share = jax.nn.sigmoid(values)
    return values * share, share


TAPS = 4
BIAS_ROW, STEP_ROW, SKIP_ROW = 4, 5, 6


def front_kernel(tokens_ref, gain_ref, w_ref, rows_ref, xproj_ref, mask_ref, inner_ref, pre_ref, u_ref, dbc_ref, xn_ref, xnt_ref):
    @pl.when(pl.program_id(0) == 0)
    def _():
        x = tokens_ref[...].astype(jnp.float32)
        inv = lax.rsqrt(jnp.mean(x * x, axis=1, keepdims=True) + EPSILON)
        xn = (x * inv * gain_ref[...]).astype(jnp.bfloat16)
        xn_ref[...] = xn
        xnt_ref[...] = xn.T
        dbc_ref[...] = jnp.zeros_like(dbc_ref)

    inner = dot(xn_ref[...], w_ref[...])
    rows = rows_ref[...]
    pre = block_rows(rows, BIAS_ROW, 1) + block_rows(rows, TAPS - 1, 1) * inner
    for offset in range(1, TAPS):
        shifted = pltpu.roll(inner, offset, 0) * mask_ref[:, offset : offset + 1]
        pre = pre + block_rows(rows, TAPS - 1 - offset, 1) * shifted
    u = smooth(pre)[0].astype(jnp.bfloat16)
    inner_ref[...] = inner.astype(inner_ref.dtype)
    pre_ref[...] = pre
    u_ref[...] = u
    dbc_ref[...] += transposed_product(u, xproj_ref[...])


def whole_spec(shape):
    return pl.BlockSpec(shape, lambda i: (0,) * len(shape))


def columns_spec(rows, block):
    return pl.BlockSpec((rows, block), lambda i: (0, i))


def rows_spec(block, columns):
    return pl.BlockSpec((block, columns), lambda i: (i, 0))


def front(tokens, gain, inner_w, by_channel, xproj_t, masks, block=256):
    length, features = tokens.shape
    width = inner_w.shape[1]
    low, wide = jnp.bfloat16, jnp.float32
    return pl.pallas_call(
        front_kernel,
        grid=(width // block,),
        in_specs=[
            whole_spec(tokens.shape),
            whole_spec(gain.shape),
            columns_spec(features, block),
            columns_spec(by_channel.shape[0], block),
            columns_spec(LANES, block),
            whole_spec(masks.shape),
        ],
        out_specs=[
            columns_spec(length, block),
            columns_spec(length, block),
            columns_spec(length, block),
            whole_spec((length, LANES)),
            whole_spec((length, features)),
            whole_spec((features, length)),
        ],
        out_shape=[
            jax.ShapeDtypeStruct((length, width), low),
            jax.ShapeDtypeStruct((length, width), wide),
            jax.ShapeDtypeStruct((length, width), low),
            jax.ShapeDtypeStruct((length, LANES), wide),
            jax.ShapeDtypeStruct((length, features), low),
            jax.ShapeDtypeStruct((features, length), low),
        ],
        compiler_params=pltpu.CompilerParams(vmem_limit_bytes=48 << 20),
        name="front",
    )(tokens, gain, inner_w, by_channel, xproj_t, masks)


def spread_states(dbc, first, states):
    rows = QLEN * states
    repeated = jnp.broadcast_to(dbc[:, None, :], (QLEN, states, LANES)).reshape(rows, LANES)
    state = lax.broadcasted_iota(jnp.int32, (rows, LANES), 0) % states
    own = jnp.where(lane_index((rows, LANES)) == first + state, repeated, 0.0)
    return jnp.broadcast_to(jnp.sum(own, axis=1, keepdims=True), (rows, LANES))


def diagonal_states(dbc, first, states):
    rows = QLEN * states
    pick = (
        lax.broadcasted_iota(jnp.int32, (LANES, rows), 0) == first + lane_index((LANES, rows)) % states
    ).astype(jnp.bfloat16)
    tiled = dot(dbc.astype(jnp.bfloat16), pick)
    own = lane_index((QLEN, rows)) // states == lax.broadcasted_iota(jnp.int32, (QLEN, rows), 0)
    return jnp.where(own, tiled, 0.0).astype(jnp.bfloat16)


def step_rank(dbc, rank):
    return jnp.where(lane_index(dbc.shape) < rank, dbc, 0.0).astype(jnp.bfloat16)


def twice(values):
    return jnp.concatenate([values] * (WIDE // LANES), axis=1)


def forward_kernel(rank, group, count, u_ref, dbc_ref, mask_ref, rows_ref, dtproj_ref, rate_ref, *refs):
    shards, (y_ref, h_ref, dt_ref), outs = refs[:count], refs[count : count + 3], refs[count + 3 : 2 * count + 3]
    (state, long_s, feed_s, b_s, cblk_s), scratch = refs[2 * count + 3 : 2 * count + 8], refs[2 * count + 8 :]
    blocks, _, width = long_s.shape
    states = rate_ref.shape[0]
    span = QLEN * states
    gather = Gather(shards, outs, scratch)
    run_stages(gather.stages[:-1], FORWARD_STEPS)

    @pl.when(pl.program_id(0) == 0)
    def _():
        state[...] = jnp.zeros_like(state)

    rank_rows = step_rank(dbc_ref[...], rank)
    keep = mask_ref[:, 1:2] > 0
    for c in range(0, width, WIDE):
        s = slice(c, c + WIDE)
        dt = jax.nn.softplus(dot(rank_rows, dtproj_ref[:, s]) + rows_ref[STEP_ROW : STEP_ROW + 1, s])
        dt_ref[:, s] = dt
        long = jnp.where(keep, dt, NEVER)
        feed = dt * u_ref[:, s].astype(jnp.float32)
        for j in range(blocks):
            long_s[j, :, s] = long[j * QLEN : (j + 1) * QLEN]
            feed_s[j, :, s] = feed[j * QLEN : (j + 1) * QLEN]
    for j in range(blocks):
        dbc = dbc_ref[j * QLEN : (j + 1) * QLEN, :]
        b_s[j * span : (j + 1) * span, :] = spread_states(dbc, rank, states)
        cblk_s[j * QLEN : (j + 1) * QLEN, :] = diagonal_states(dbc, rank + states, states)

    def block(j, carried):
        r0 = pl.multiple_of(j * QLEN, QLEN)
        h0 = pl.multiple_of(j * span, span)
        for c0 in range(0, width, group * WIDE):
            columns = [slice(c, c + WIDE) for c in range(c0, c0 + group * WIDE, WIDE)]
            held = [state[:, s] for s in columns]
            rates = [rate_ref[:, s] for s in columns]
            for t in range(QLEN):
                b_t = twice(b_s[pl.ds(h0 + t * states, states), :])
                for k, s in enumerate(columns):
                    decay = jnp.exp2(long_s[j, t : t + 1, s] * rates[k])
                    held[k] = decay * held[k] + b_t * feed_s[j, t : t + 1, s]
                    h_ref[pl.ds(h0 + t * states, states), s] = held[k].astype(h_ref.dtype)
            for k, s in enumerate(columns):
                state[:, s] = held[k]
            s = slice(c0, c0 + group * WIDE)
            y_ref[pl.ds(r0, QLEN), s] = dot(cblk_s[pl.ds(r0, QLEN), :], h_ref[pl.ds(h0, span), s])
        return carried

    lax.fori_loop(0, blocks, block, 0)
    run_stages(gather.stages[-1:], (pl.num_programs(0) - 1,))


def scan_forward(rank, u, dbc, masks, by_channel, dtproj, rate2, shards, collective_id, blocks=2, group=2):
    count = len(shards)
    anywhere = [pl.BlockSpec(memory_space=pl.ANY)] * count
    tokens, width = u.shape
    states = rate2.shape[0]
    rows = blocks * QLEN
    y, h, dt, *gathered = pl.pallas_call(
        functools.partial(forward_kernel, rank, group, count),
        grid=(tokens // rows,),
        in_specs=[
            rows_spec(rows, width),
            rows_spec(rows, LANES),
            rows_spec(rows, masks.shape[1]),
            whole_spec(by_channel.shape),
            whole_spec(dtproj.shape),
            whole_spec(rate2.shape),
            *anywhere,
        ],
        out_specs=[rows_spec(rows, width), rows_spec(rows * states, width), rows_spec(rows, width), *anywhere],
        out_shape=[
            jax.ShapeDtypeStruct((tokens, width), jnp.float32),
            jax.ShapeDtypeStruct((tokens * states, width), jnp.bfloat16),
            jax.ShapeDtypeStruct((tokens, width), jnp.float32),
            *(gathered_shape(s) for s in shards),
        ],
        scratch_shapes=[
            pltpu.VMEM((states, width), jnp.float32),
            pltpu.VMEM((blocks, QLEN, width), jnp.float32),
            pltpu.VMEM((blocks, QLEN, width), jnp.float32),
            pltpu.VMEM((rows * states, LANES), jnp.float32),
            pltpu.VMEM((rows, QLEN * states), jnp.bfloat16),
            *Gather.scratch(shards),
        ],
        compiler_params=pltpu.CompilerParams(
            collective_id=collective_id, has_side_effects=True, vmem_limit_bytes=48 << 20
        ),
        name="scan_forward",
    )(u, dbc, masks, by_channel, dtproj, rate2, *shards)
    return y, h, dt, gathered


def middle_kernel(
    xn_ref, xnt_ref, gate_ref, y_ref, u_ref, rows_ref, out_ref, cot_ref, tokens_ref, mask_ref,
    mixed_ref, dy_ref, dgate_ref, outgrad_ref, gategrad_ref, skip_ref, dxn_ref, branch, dbranch
):
    live = mask_ref[:, 0:1]

    @pl.when(pl.program_id(0) == 0)
    def _():
        branch[...] = jnp.zeros_like(branch)
        dxn_ref[...] = jnp.zeros_like(dxn_ref)
        dbranch[...] = (live * cot_ref[...].astype(jnp.float32)).astype(jnp.bfloat16)

    gate = dot(xn_ref[...], gate_ref[...])
    opened, share = smooth(gate)
    u = u_ref[...].astype(jnp.float32)
    y = y_ref[...] + rows_ref[SKIP_ROW : SKIP_ROW + 1, :] * u
    gated = (y * opened).astype(jnp.bfloat16)
    d_branch = dbranch[...]
    branch[...] += dot(gated, out_ref[...])
    outgrad_ref[...] = rows_product(gated, d_branch).astype(outgrad_ref.dtype)
    d_gated = transposed_product(d_branch, out_ref[...])
    d_y = d_gated * opened
    dy_ref[...] = d_y
    skip_ref[...] = jnp.sum(d_y * u, axis=0, keepdims=True)
    d_gate = (d_gated * y * share * (1.0 + gate * (1.0 - share))).astype(jnp.bfloat16)
    dgate_ref[...] = d_gate
    gategrad_ref[...] = dot(xnt_ref[...], d_gate).astype(gategrad_ref.dtype)
    dxn_ref[...] += transposed_product(d_gate, gate_ref[...])

    @pl.when(pl.program_id(0) == pl.num_programs(0) - 1)
    def _():
        mixed_ref[...] = (tokens_ref[...].astype(jnp.float32) + live * branch[...]).astype(mixed_ref.dtype)


def middle(xn, xnt, gate_w, y, u, by_channel, out_w, cotangent, tokens, masks, block=256):
    length, features = tokens.shape
    width = gate_w.shape[1]
    low, wide = jnp.bfloat16, jnp.float32
    channels = columns_spec(length, block)
    return pl.pallas_call(
        middle_kernel,
        grid=(width // block,),
        in_specs=[
            whole_spec(xn.shape),
            whole_spec(xnt.shape),
            columns_spec(features, block),
            channels,
            channels,
            columns_spec(by_channel.shape[0], block),
            rows_spec(block, features),
            whole_spec(tokens.shape),
            whole_spec(tokens.shape),
            whole_spec(masks.shape),
        ],
        out_specs=[
            whole_spec(tokens.shape),
            channels,
            channels,
            rows_spec(block, features),
            columns_spec(features, block),
            columns_spec(1, block),
            whole_spec(tokens.shape),
        ],
        out_shape=[
            jax.ShapeDtypeStruct(tokens.shape, low),
            jax.ShapeDtypeStruct((length, width), wide),
            jax.ShapeDtypeStruct((length, width), low),
            jax.ShapeDtypeStruct((width, features), low),
            jax.ShapeDtypeStruct((features, width), low),
            jax.ShapeDtypeStruct((1, width), wide),
            jax.ShapeDtypeStruct(tokens.shape, wide),
        ],
        scratch_shapes=[pltpu.VMEM(tokens.shape, wide), pltpu.VMEM(tokens.shape, low)],
        compiler_params=pltpu.CompilerParams(vmem_limit_bytes=56 << 20),
        name="middle",
    )(xn, xnt, gate_w, y, u, by_channel, out_w, cotangent, tokens, masks)


def backward_kernel(rank, count, u_ref, dt_ref, dy_ref, dbc_ref, mask_ref, h_ref, before_ref, rows_ref, dtproj_ref, rate2_ref, rate_ref, *refs):
    grads, (du_ref, ddbc_ref, ldt_ref, dtproj_grad, bias_grad) = refs[:count], refs[count : count + 5]
    outs, refs = refs[count + 5 : 2 * count + 5], refs[2 * count + 5 :]
    message, long_s, feed_s, c_s, bblk_s, g_s, lrate_s, db_s, dc_s, before_s, e_s, lsum_s, small_s = refs[:13]
    blocks, _, width = dt_ref.shape
    states = rate_ref.shape[0]
    span = QLEN * states
    low, wide = jnp.bfloat16, jnp.float32
    reduction = Reduction(grads, outs, refs[13:])
    early = len(BACKWARD_STEPS)
    run_stages(reduction.stages[:early], BACKWARD_STEPS)

    @pl.when(pl.program_id(0) == 0)
    def _():
        message[...] = jnp.zeros_like(message)
        ldt_ref[...] = jnp.zeros_like(ldt_ref)
        dtproj_grad[...] = jnp.zeros_like(dtproj_grad)
        bias_grad[...] = jnp.zeros_like(bias_grad)

    for j in range(blocks):
        own = slice(j * QLEN, (j + 1) * QLEN)
        keep = mask_ref[own, 1:2] > 0
        for c in range(0, width, WIDE):
            s = slice(c, c + WIDE)
            dt = dt_ref[j, :, s]
            long_s[j, :, s] = jnp.where(keep, dt, NEVER)
            feed_s[j, :, s] = dt * u_ref[own, s].astype(wide)
        dbc = dbc_ref[own, :]
        c_s[j * span : (j + 1) * span, :] = spread_states(dbc, rank + states, states)
        bblk_s[own, :] = diagonal_states(dbc, rank, states)
    by_token = (
        lane_index((QLEN, span)) // states == lax.broadcasted_iota(jnp.int32, (QLEN, span), 0)
    ).astype(low)
    state_of = lax.broadcasted_iota(jnp.int32, (span, LANES), 0) % states
    at_b = lane_index((span, LANES)) == rank + state_of
    at_c = lane_index((span, LANES)) == rank + states + state_of

    def block(step, carried):
        j = blocks - 1 - step
        r0 = pl.multiple_of(j * QLEN, QLEN)
        h0 = pl.multiple_of(j * span, span)

        @pl.when(j == 0)
        def _():
            before_s[...] = before_ref[...]

        @pl.when(j > 0)
        def _():
            before_s[...] = h_ref[pl.ds(pl.multiple_of(jnp.maximum(h0 - states, 0), states), states), :]

        db_s[...] = jnp.zeros_like(db_s)
        dc_s[...] = jnp.zeros_like(dc_s)
        for c in range(0, width, WIDE):
            s = slice(c, c + WIDE)
            held, rate2, rate, total = message[:, s], rate2_ref[:, s], rate_ref[:, s], ldt_ref[:, s]
            pending = None
            now = h_ref[pl.ds(h0 + (QLEN - 1) * states, states), s]
            for t in reversed(range(QLEN)):
                at = slice(t * states, (t + 1) * states)
                d_y = jnp.broadcast_to(dy_ref[j, t : t + 1, s], (states, WIDE))
                g = twice(c_s[pl.ds(h0 + t * states, states), :]) * d_y + held
                g_low = g.astype(low)
                g_s[at, s] = g_low
                dt = jnp.broadcast_to(long_s[j, t : t + 1, s], (states, WIDE))
                held = jnp.exp2(dt * rate2) * g
                before = before_s[:, s] if t == 0 else h_ref[pl.ds(h0 + (t - 1) * states, states), s]
                l = held.astype(low) * before
                lrate_s[at, s] = l * rate
                ldt = l * dt.astype(low)
                if pending is None:
                    pending = ldt
                else:
                    total = total + (pending + ldt).astype(wide)
                    pending = None
                feed = jnp.broadcast_to(feed_s[j, t : t + 1, s], (states, WIDE))
                for sums, product in ((db_s, g_low * feed.astype(low)), (dc_s, now * d_y.astype(low))):
                    sums[at, :] += (product[:, :LANES] + product[:, LANES:]).astype(wide)
                now = before
            message[:, s] = held
            ldt_ref[:, s] = total
            e_s[pl.ds(r0, QLEN), s] = dot(bblk_s[pl.ds(r0, QLEN), :], g_s[:, s])
            lsum_s[pl.ds(r0, QLEN), s] = dot(by_token, lrate_s[:, s])
        d_b = jnp.sum(db_s[...], axis=1, keepdims=True)
        d_c = jnp.sum(dc_s[...], axis=1, keepdims=True)
        placed = jnp.where(at_b, d_b, jnp.where(at_c, d_c, 0.0)).astype(low)
        small_s[pl.ds(r0, QLEN), :] = dot(by_token, placed)
        return carried

    lax.fori_loop(0, blocks, block, 0)
    rank_rows = step_rank(dbc_ref[...], rank)
    d_rank = jnp.zeros(rank_rows.shape, wide)
    tokens = blocks * QLEN
    for c in range(0, width, WIDE):
        s = slice(c, c + WIDE)
        dt = dt_ref[:, :, s].reshape(tokens, WIDE)
        d_y = dy_ref[:, :, s].reshape(tokens, WIDE)
        e = e_s[:, s]
        share = jnp.where(dt < 0.01, dt * (1.0 - dt * (0.5 - dt * (1.0 / 6.0))), 1.0 - jnp.exp(-dt))
        d_dt = e * u_ref[:, s].astype(wide) + lsum_s[:, s]
        d_step = (d_dt * share).astype(low)
        bias_grad[:, s] += jnp.sum(d_step.astype(wide), axis=0, keepdims=True)
        dtproj_grad[:, s] += rows_product(rank_rows, d_step)
        d_rank += transposed_product(d_step, dtproj_ref[:, s])
        du_ref[:, s] = d_y * rows_ref[SKIP_ROW : SKIP_ROW + 1, s] + e * dt
    ddbc_ref[...] = (jnp.where(lane_index(d_rank.shape) < rank, d_rank, 0.0) + small_s[...]).astype(low)
    late = reduction.stages[early:]
    run_stages(late, (pl.num_programs(0) - 1,) * len(late))


def scan_backward(rank, u, dt, d_y, dbc, masks, h, by_channel, dtproj, rate2, rate, grads, collective_id, blocks=2):
    count = len(grads)
    anywhere = [pl.BlockSpec(memory_space=pl.ANY)] * count
    tokens, width = u.shape
    states = rate2.shape[0]
    rows = blocks * QLEN
    steps = tokens // rows
    low, wide = jnp.bfloat16, jnp.float32
    back = lambda i: (steps - 1 - i, 0)
    flat = lambda columns: pl.BlockSpec((rows, columns), back)
    cubes = pl.BlockSpec((blocks, QLEN, width), lambda i: (steps - 1 - i, 0, 0))
    in_blocks = lambda v: v.reshape(tokens // QLEN, QLEN, width)
    du, ddbc, ldt, dtproj_grad, bias_grad, *sums = pl.pallas_call(
        functools.partial(backward_kernel, rank, count),
        grid=(steps,),
        in_specs=[
            flat(width),
            cubes,
            cubes,
            flat(LANES),
            flat(masks.shape[1]),
            pl.BlockSpec((rows * states, width), back),
            pl.BlockSpec((states, width), lambda i: (jnp.maximum((steps - 1 - i) * rows - 1, 0), 0)),
            whole_spec(by_channel.shape),
            whole_spec(dtproj.shape),
            whole_spec(rate2.shape),
            whole_spec(rate.shape),
            *anywhere,
        ],
        out_specs=[
            flat(width),
            flat(LANES),
            whole_spec(rate2.shape),
            whole_spec(dtproj.shape),
            whole_spec((1, width)),
            *anywhere,
        ],
        out_shape=[
            jax.ShapeDtypeStruct((tokens, width), wide),
            jax.ShapeDtypeStruct((tokens, LANES), low),
            jax.ShapeDtypeStruct(rate2.shape, wide),
            jax.ShapeDtypeStruct(dtproj.shape, wide),
            jax.ShapeDtypeStruct((1, width), wide),
            *(jax.ShapeDtypeStruct(g.shape[1:], g.dtype) for g in grads),
        ],
        scratch_shapes=[
            pltpu.VMEM((states, width), wide),
            pltpu.VMEM((blocks, QLEN, width), wide),
            pltpu.VMEM((blocks, QLEN, width), wide),
            pltpu.VMEM((rows * states, LANES), wide),
            pltpu.VMEM((rows, QLEN * states), low),
            pltpu.VMEM((QLEN * states, width), low),
            pltpu.VMEM((QLEN * states, width), low),
            pltpu.VMEM((QLEN * states, LANES), wide),
            pltpu.VMEM((QLEN * states, LANES), wide),
            pltpu.VMEM((states, width), low),
            pltpu.VMEM((rows, width), wide),
            pltpu.VMEM((rows, width), wide),
            pltpu.VMEM((rows, LANES), wide),
            *Reduction.scratch(grads),
        ],
        compiler_params=pltpu.CompilerParams(
            collective_id=collective_id, has_side_effects=True, vmem_limit_bytes=56 << 20
        ),
        name="scan_backward",
    )(u, in_blocks(dt), in_blocks(d_y), dbc, masks, h, h, by_channel, dtproj, rate2, rate, *grads)
    return du, ddbc, ldt, dtproj_grad, bias_grad, sums


def tail_kernel(
    du_ref, ddbc_ref, xproj_ref, u_ref, inner_ref, pre_ref, rows_ref, mask_ref, xnt_ref, w_ref, dgate_ref, tokens_ref, cot_ref, gain_ref,
    innergrad_ref, xprojgrad_ref, rowgrad_ref, tokengrad_ref, gaingrad_ref, dxn
):
    wide = jnp.float32

    @pl.when(pl.program_id(0) == 0)
    def _():
        dxn[...] = dgate_ref[...]

    rows = rows_ref[...]
    pre = pre_ref[...]
    share = jax.nn.sigmoid(pre)
    d_u = du_ref[...] + dot(ddbc_ref[...], xproj_ref[...])
    d_pre = d_u * share * (1.0 + pre * (1.0 - share))
    inner = inner_ref[...].astype(wide)
    d_inner = block_rows(rows, TAPS - 1, 1) * d_pre
    sums = [None] * 8
    sums[TAPS - 1] = jnp.sum(d_pre * inner, axis=0, keepdims=True)
    sums[BIAS_ROW] = jnp.sum(d_pre, axis=0, keepdims=True)
    for offset in range(1, TAPS):
        same = d_pre * mask_ref[:, offset : offset + 1]
        back = pltpu.roll(same, same.shape[0] - offset, 0)
        sums[TAPS - 1 - offset] = jnp.sum(back * inner, axis=0, keepdims=True)
        d_inner = d_inner + block_rows(rows, TAPS - 1 - offset, 1) * back
    nothing = jnp.zeros_like(sums[0])
    rowgrad_ref[...] = jnp.concatenate([nothing if v is None else v for v in sums], axis=0)
    xprojgrad_ref[...] = rows_product(ddbc_ref[...], u_ref[...])
    d_inner = d_inner.astype(jnp.bfloat16)
    innergrad_ref[...] = dot(xnt_ref[...], d_inner).astype(innergrad_ref.dtype)
    dxn[...] += transposed_product(d_inner, w_ref[...])

    @pl.when(pl.program_id(0) == pl.num_programs(0) - 1)
    def _():
        x = tokens_ref[...].astype(wide)
        inv = lax.rsqrt(jnp.mean(x * x, axis=1, keepdims=True) + EPSILON)
        x_hat = x * inv
        gaingrad_ref[...] = jnp.sum(dxn[...] * x_hat, axis=0, keepdims=True)
        d_hat = dxn[...] * gain_ref[...]
        level = jnp.mean(d_hat * x_hat, axis=1, keepdims=True)
        tokengrad_ref[...] = cot_ref[...].astype(wide) + inv * (d_hat - x_hat * level)


def tail(du, ddbc, xproj_t, u, inner, pre, by_channel, masks, xnt, inner_w, dxn_gate, tokens, cotangent, gain, block=256):
    length, features = tokens.shape
    width = inner_w.shape[1]
    low, wide = jnp.bfloat16, jnp.float32
    channels = columns_spec(length, block)
    return pl.pallas_call(
        tail_kernel,
        grid=(width // block,),
        in_specs=[
            channels,
            whole_spec(ddbc.shape),
            columns_spec(LANES, block),
            channels,
            channels,
            channels,
            columns_spec(by_channel.shape[0], block),
            whole_spec(masks.shape),
            whole_spec(xnt.shape),
            columns_spec(features, block),
            whole_spec(dxn_gate.shape),
            whole_spec(tokens.shape),
            whole_spec(tokens.shape),
            whole_spec(gain.shape),
        ],
        out_specs=[
            columns_spec(features, block),
            columns_spec(LANES, block),
            columns_spec(8, block),
            whole_spec(tokens.shape),
            whole_spec((1, features)),
        ],
        out_shape=[
            jax.ShapeDtypeStruct((features, width), low),
            jax.ShapeDtypeStruct((LANES, width), wide),
            jax.ShapeDtypeStruct((8, width), wide),
            jax.ShapeDtypeStruct(tokens.shape, wide),
            jax.ShapeDtypeStruct((1, features), wide),
        ],
        scratch_shapes=[pltpu.VMEM(tokens.shape, wide)],
        compiler_params=pltpu.CompilerParams(vmem_limit_bytes=56 << 20),
        name="tail",
    )(du, ddbc, xproj_t, u, inner, pre, by_channel, masks, xnt, inner_w, dxn_gate, tokens, cotangent, gain)


def add_groups(sums):
    groups = lax.axis_size("dp") // GROUP
    if groups == 1:
        return sums
    alike = [[g * GROUP + i for g in range(groups)] for i in range(GROUP)]
    return lax.psum(sums, "dp", axis_index_groups=alike)


def body(
    tokens,
    cotangent,
    prot_lens,
    clus_start,
    norm_gain,
    in_w,
    conv_w,
    conv_b,
    xproj_w,
    dtproj_w,
    dt_bias,
    a_log,
    d_skip,
    out_w,
):
    length = tokens.shape[0]
    features = norm_gain.shape[0]
    width = in_w.shape[1] // 2
    rank, owned = dtproj_w.shape
    states = a_log.shape[0]
    live_mask, same_masks = protein_masks(prot_lens[0], clus_start[0], length, TAPS)
    masks = jnp.stack([live_mask, *same_masks], axis=1)
    fill = lambda v: jnp.pad(v, ((0, 0), (0, owned - v.shape[1])))
    packed = jnp.concatenate(
        [dtproj_w, a_log, xproj_w.T, conv_w, conv_b[None], dt_bias[None], d_skip[None], fill(norm_gain[None])], axis=0
    )
    used = packed.shape[0]
    packed = jnp.pad(packed, ((0, -used % LANES), (0, 0)))
    inner_w, packed = gather_weights((in_w[:, :width], packed), 1)
    inner_w = inner_w.reshape(-1, width)
    gain = packed[:, used - 1, :features].reshape(1, -1).astype(jnp.float32)
    packed = jnp.swapaxes(packed, 0, 1).reshape(packed.shape[1], -1)
    dtproj = packed[:LANES]
    decay_rate = -jnp.exp(packed[rank : rank + states].astype(jnp.float32))
    rate2 = decay_rate * LOG2E
    xproj_t = packed[rank + states : rank + states + LANES]
    by_channel = packed[used - 8 : used].astype(jnp.float32)
    inner, pre, u, dbc, xn, xnt = front(tokens, gain, inner_w, by_channel, xproj_t, masks)
    y, h, dt, (gate_w, out_full) = scan_forward(
        rank, u, dbc, masks, by_channel, dtproj, rate2, (in_w[:, width:], out_w), 2
    )
    gate_w = gate_w.reshape(-1, width)
    out_full = out_full.reshape(-1, out_full.shape[2])
    mixed, d_y, _, out_local, gate_local, skip_local, dxn_gate = middle(
        xn, xnt, gate_w, y, u, by_channel, out_full, cotangent, tokens, masks
    )
    in_pieces = lambda v: v.reshape((4, 2, 2, 2, v.shape[0] // 32, v.shape[1]))
    du, ddbc, ldt, dtproj_local, dtb_local, early_sums = scan_backward(
        rank,
        u,
        dt,
        d_y,
        dbc,
        masks,
        h,
        by_channel,
        dtproj,
        rate2,
        decay_rate.astype(jnp.bfloat16),
        [in_pieces(gate_local), in_pieces(out_local)],
        3,
    )
    inner_local, xproj_local, row_local, token_grad, gain_local = tail(
        du, ddbc, xproj_t, u, inner, pre, by_channel, masks, xnt, inner_w, dxn_gate, tokens, cotangent, gain
    )
    small_local = jnp.concatenate(
        [
            dtproj_local[:rank],
            ldt * decay_rate,
            xproj_local[: xproj_w.shape[1]],
            row_local[: TAPS + 1],
            dtb_local,
            skip_local,
            fill(gain_local.reshape(4, -1)).reshape(1, -1),
        ],
        axis=0,
    ).astype(jnp.bfloat16)
    small_local = jnp.pad(small_local, ((0, -used % LANES), (0, 0)))
    small_local = jnp.swapaxes(small_local.reshape(small_local.shape[0], 4, owned), 0, 1)
    small_local = small_local.reshape(4, 2, 2, 2, -1, owned)
    late_sums = reduce_gradients([in_pieces(inner_local), small_local], 4)
    in_rows = lambda v: v.reshape(-1, v.shape[-1]).astype(jnp.float32)
    gate_grad, out_grad, inner_grad, small = add_groups([in_rows(v) for v in (*early_sums, *late_sums)])
    in_grad = jnp.concatenate([inner_grad, gate_grad], axis=1)
    dtproj_grad, alog_grad, xproj_grad = small[:rank], small[rank : rank + states], small[rank + states : used - 8].T
    conv_grad, convb_grad, dtb_grad, skip_grad = small[used - 8 : used - 4], small[used - 4], small[used - 3], small[used - 2]
    return (
        mixed,
        token_grad,
        small[used - 1, :features],
        in_grad,
        conv_grad,
        convb_grad,
        xproj_grad,
        dtproj_grad,
        dtb_grad,
        alog_grad,
        skip_grad,
        out_grad,
    )


def solution(mesh):
    in_specs = (
        P(("dp", "fsdp"), None),
        P(("dp", "fsdp"), None),
        P(("dp", "fsdp"), None),
        P(("dp", "fsdp"), None),
        P("fsdp"),
        P("fsdp", None),
        P(None, "fsdp"),
        P("fsdp"),
        P("fsdp", None),
        P(None, "fsdp"),
        P("fsdp"),
        P(None, "fsdp"),
        P("fsdp"),
        P("fsdp", None),
    )
    out_specs = (
        P(("dp", "fsdp"), None),
        P(("dp", "fsdp"), None),
        P("fsdp"),
        P("fsdp", None),
        P(None, "fsdp"),
        P("fsdp"),
        P("fsdp", None),
        P(None, "fsdp"),
        P("fsdp"),
        P(None, "fsdp"),
        P("fsdp"),
        P("fsdp", None),
    )
    return jax.shard_map(body, mesh=mesh, in_specs=in_specs, out_specs=out_specs, check_vma=False)
```

profile of v0, /device:TPU:0, one launch (start us, length us, event | category | flops | bytes accessed | tf_op | source)
XLA Modules:
  0.0 307.7 jit_solution(2125993979993963499)
XLA Ops:
  0.6 0.0 copy-start.25
  0.7 0.0 copy-start.22
  0.7 0.0 copy-start.23
  0.7 0.0 copy-start.24
  0.7 0.0 copy-start.17
  0.7 0.0 copy-start.21
  0.7 0.0 copy-start.18
  0.7 0.9 reduce-window.4
  1.6 0.7 fusion.3
  2.3 0.7 and_bitcast_fusion
  3.0 0.1 convert_reduce_fusion
  3.0 0.1 fusion.1
  3.1 0.6 slice.83
  3.7 0.7 compare_and_fusion
  4.5 0.2 copy.44
  4.7 0.0 copy-start.2
  4.7 0.0 copy-start.3
  4.7 1.8 fusion.4
  6.5 0.0 copy-done.25
  6.5 0.0 copy-done.22
  6.6 0.0 copy-done.23
  6.6 0.0 copy-done.24
  6.6 0.0 copy-done.17
  6.6 0.0 copy-done.21
  6.6 3.4 %concatenate.31 = bf16[184,512]{1,0:T(8,128)(2,1)} concatenate(bf16[64,512]{1,0:T(8,128)(2,1)} %param.23, bf16[16,512]{1,0:T(8,128)(2,1)S(1)} %copy-done.18, bf16[96,512]{1,0:T(8,128)(2,1)S(1)} %bitcast.87, bf16[4,512]{1,0:T(4,128)(2,1)S(1)} %copy-done.21, bf16[1,512]{1,0:T(2,128)(2,1)S(1)} %broadcast_in_dim.15, bf16[1,512]{1,0:T(2,128)(2,1)S(1)} %broadcast_in_dim.16, ...), dimensions={0} | concatenate | bytes 376832 | tf_op jit(solution)/shard_map/concatenate | solution.py:1022
  10.0 0.9 pad.20.refs_1_
  10.9 23.3 %gather_weights.1 = (bf16[4,256,2048]{2,1,0:T(8,128)(2,1)S(1)}, bf16[4,256,512]{2,1,0:T(8,128)(2,1)S(1)}) custom-call(bf16[256,2048]{1,0:T(8,128)(2,1)S(1)} %get-tuple-element.79.refs_0_, bf16[256,512]{1,0:T(8,128)(2,1)S(1)} %pad.20.refs_1_), custom_call_target="tpu_custom_call" | custom-call | tf_op jit(solution)/shard_map/gather_weights/pallas_call | solution.py:234
  34.2 0.0 copy-start.1
  34.3 2.0 copy-done.1
  36.3 0.0 copy-start.7
  36.3 0.1 slice_bitcast_fusion
  36.5 0.0 copy-start.11
  36.5 0.0 copy-start.12
  36.5 11.5 %front.1 = (bf16[512,2048]{1,0:T(8,128)(2,1)}, f32[512,2048]{1,0:T(8,128)}, bf16[512,2048]{1,0:T(8,128)(2,1)}, f32[512,128]{1,0:T(8,128)S(1)}, bf16[512,1024]{1,...) custom-call(bf16[512,1024]{1,0:T(8,128)(2,1)S(1)} %copy-done.3, f32[1,1024]{1,0:T(1,128)S(1)} %convert.46.gain_ref, ...), custom_call_target="tpu_custom_call" | custom-call | tf_op jit(solution)/shard_map/front/pallas_call | solution.py:496
  48.1 0.0 copy-start.8
  48.2 0.8 copy-done.6
  49.0 0.0 copy-done.2
  49.0 0.0 copy-done.11
  49.0 1.6 copy-done
  50.6 43.7 %scan_forward.1 = (f32[512,2048]{1,0:T(8,128)}, bf16[8192,2048]{1,0:T(8,128)(2,1)}, f32[512,2048]{1,0:T(8,128)}, bf16[4,256,2048]{2,1,0:T(8,128)(2,1)}, bf16[4,512,1024]{2,1,0:T(8,128)(2,1)}) custom-call(bf16[512,2048]{1,0:T(8,128)(2,1)S(1)} %copy-done, f32[512,128]{1,0:T(8,128)S(1)} %get-tuple-element.50.dbc_ref, f32[512,4]{1,0:T(8,128)S(1)} %stack.18.mask_ref, ...), custom_call_target="tpu_custom_call" | custom-call | tf_op jit(solution)/shard_map/scan_forward/pallas_call | solution.py:612
  94.3 27.3 %middle.1 = (bf16[512,1024]{1,0:T(8,128)(2,1)}, f32[512,2048]{1,0:T(8,128)}, bf16[512,2048]{1,0:T(8,128)(2,1)}, bf16[2048,1024]{1,0:T(8,128)(2,1)}, bf16[1024,20...) custom-call(bf16[512,1024]{1,0:T(8,128)(2,1)} %copy-done.10, bf16[1024,512]{1,0:T(8,128)(2,1)} %copy-done.6, ...), custom_call_target="tpu_custom_call" | custom-call | tf_op jit(solution)/shard_map/middle/pallas_call | solution.py:686
  121.7 0.6 convert_element_type.73.rate_ref
  122.4 93.7 %scan_backward.1 = (f32[512,2048]{1,0:T(8,128)}, bf16[512,128]{1,0:T(8,128)(2,1)}, f32[16,2048]{1,0:T(8,128)}, f32[128,2048]{1,0:T(8,128)}, f32[1,2048]{1,0:T(1,...) custom-call(bf16[512,2048]{1,0:T(8,128)(2,1)} %get-tuple-element.49.u_ref, ...), custom_call_target="tpu_custom_call" | custom-call | tf_op jit(solution)/shard_map/scan_backward/pallas_call | solution.py:846
  216.1 0.0 copy-start.16
  216.1 0.0 copy-start.20
  216.1 0.0 copy-start.19
  216.1 18.8 %tail.1 = (bf16[1024,2048]{1,0:T(8,128)(2,1)}, f32[128,2048]{1,0:T(8,128)}, f32[8,2048]{1,0:T(8,128)}, f32[512,1024]{1,0:T(8,128)}, f32[1,1024]{1,0:T(1,128)}) custom-call(f32[512,2048]{1,0:T(8,128)} %get-tuple-element.60.du_ref, bf16[512,128]{1,0:T(8,128)(2,1)} %get-tuple-element.61.ddbc_ref, bf16[128,2048]{1,0:T(8,128)(2,1)} %bitcast.68, ...), custom_call_target="tpu_custom_call" | custom-call | tf_op jit(solution)/shard_map/tail/pallas_call | solution.py:951
  234.9 1.2 slice.124
  236.1 0.8 slice.126
  237.0 0.7 convert_reduce_fusion.1
  237.7 1.1 slice.125
  238.8 0.3 concatenate.36
  239.1 0.1 pad.22
  239.2 1.1 copy.54
  240.3 58.0 %reduce_gradients.1 = (bf16[2,2,2,32,2048]{4,3,2,1,0:T(8,128)(2,1)}, bf16[2,2,2,32,512]{4,3,2,1,0:T(8,128)(2,1)}) custom-call(bf16[4,2,2,2,32,2048]{5,4,3,2,1,0:T(8,128)(2,1)} %bitcast.72, bf16[4,2,2,2,32,512]{5,4,3,2,1,0:T(8,128)(2,1)} %bitcast.73), custom_call_target="tpu_custom_call" | custom-call | tf_op jit(solution)/shard_map/reduce_gradients/pallas_call | solution.py:423
  298.4 3.8 %maximum_convert_fusion = f32[256,4096]{1,0:T(8,128)} fusion(bf16[256,2048]{1,0:T(8,128)(2,1)S(1)} %bitcast.84, bf16[256,2048]{1,0:T(8,128)(2,1)} %bitcast.85), kind=kLoop, calls=%fused_computation | loop fusion | flops 4194304 | bytes 6291456 | tf_op jit(solution)/shard_map/concatenate | solution.py:1082
  302.2 0.1 bitcast_convert_fusion.1
  302.3 0.7 slice_bitcast_fusion.2
  303.0 0.7 slice.113
  303.7 0.6 slice.115
  304.3 0.6 slice.110
  304.9 0.6 fusion.5
  305.5 0.6 slice.109
  306.0 1.6 bitcast_convert_fusion
  (48 shorter events, 0.4 us)
Async XLA Ops:
  0.6 5.9 %copy-start.25 = (bf16[256]{0:T(256)(128)(2,1)S(1)}, bf16[256]{0:T(256)(128)(2,1)}, u32[]{:S(2)}) copy-start(bf16[256]{0:T(256)(128)(2,1)} %param.18) | copy-start | bytes 1540
  0.7 5.9 %copy-start.22 = (bf16[512]{0:T(512)(128)(2,1)S(1)}, bf16[512]{0:T(512)(128)(2,1)}, u32[]{:S(2)}) copy-start(bf16[512]{0:T(512)(128)(2,1)} %param.21) | copy-start | bytes 3076
  0.7 5.9 %copy-start.23 = (bf16[512]{0:T(512)(128)(2,1)S(1)}, bf16[512]{0:T(512)(128)(2,1)}, u32[]{:S(2)}) copy-start(bf16[512]{0:T(512)(128)(2,1)} %param.24) | copy-start | bytes 3076
  0.7 5.9 %copy-start.24 = (bf16[512]{0:T(512)(128)(2,1)S(1)}, bf16[512]{0:T(512)(128)(2,1)}, u32[]{:S(2)}) copy-start(bf16[512]{0:T(512)(128)(2,1)} %param.26) | copy-start | bytes 3076
  0.7 5.9 %copy-start.17 = (bf16[512,96]{0,1:T(8,128)(2,1)S(1)}, bf16[512,96]{0,1:T(8,128)(2,1)}, u32[]{:S(2)}) copy-start(bf16[512,96]{0,1:T(8,128)(2,1)} %param.22) | copy-start | bytes 294916
  0.7 5.9 %copy-start.21 = (bf16[4,512]{1,0:T(4,128)(2,1)S(1)}, bf16[4,512]{1,0:T(4,128)(2,1)}, u32[]{:S(2)}) copy-start(bf16[4,512]{1,0:T(4,128)(2,1)} %param.20) | copy-start | bytes 12292
  0.7 5.9 %copy-start.18 = (bf16[16,512]{1,0:T(8,128)(2,1)S(1)}, bf16[16,512]{1,0:T(8,128)(2,1)}, u32[]{:S(2)}) copy-start(bf16[16,512]{1,0:T(8,128)(2,1)} %param.25) | copy-start | bytes 49156
  4.7 44.3 %copy-start.2 = (f32[512,4]{1,0:T(8,128)}, f32[512,4]{1,0:T(8,128)S(1)}, u32[]{:S(2)}) copy-start(f32[512,4]{1,0:T(8,128)S(1)} %stack.18.mask_ref) | copy-start | bytes 24580
  4.7 31.8 %copy-start.3 = (bf16[512,1024]{1,0:T(8,128)(2,1)S(1)}, bf16[512,1024]{1,0:T(8,128)(2,1)}, u32[]{:S(2)}) copy-start(bf16[512,1024]{1,0:T(8,128)(2,1)} %tokens_ref.5) | copy-start | bytes 3145732
  34.2 2.0 copy-start.1
  36.3 12.7 %copy-start.7 = (f32[8,2048]{1,0:T(8,128)}, f32[8,2048]{1,0:T(8,128)S(1)}, u32[]{:S(2)}) copy-start(f32[8,2048]{1,0:T(8,128)S(1)} %convert.45.rows_ref) | copy-start | bytes 196612
  36.4 57.9 %copy-start.5 = (bf16[4,16,8,512]{3,2,0,1:T(8,128)(2,1)}, bf16[4,16,8,512]{3,2,0,1:T(8,128)(2,1)S(1)}, u32[]{:S(2)}) copy-start(bf16[4,16,8,512]{3,2,0,1:T(8,128)(2,1)S(1)} %copy.49) | copy-start | bytes 1572868
  36.5 12.6 %copy-start.11 = (bf16[512,1024]{1,0:T(8,128)(2,1)S(1)}, bf16[512,1024]{1,0:T(8,128)(2,1)}, u32[]{:S(2)}) copy-start(bf16[512,1024]{1,0:T(8,128)(2,1)} %refs_1_.1) | copy-start | bytes 3145732
  36.5 57.8 %copy-start.12 = (f32[1,1024]{1,0:T(1,128)}, f32[1,1024]{1,0:T(1,128)S(1)}, u32[]{:S(2)}) copy-start(f32[1,1024]{1,0:T(1,128)S(1)} %convert.46.gain_ref) | copy-start | bytes 12292
  48.0 1.0 copy-start.6
  48.0 46.3 %copy-start.10 = (bf16[512,1024]{1,0:T(8,128)(2,1)}, bf16[512,1024]{1,0:T(8,128)(2,1)S(1)}, u32[]{:S(2)}) copy-start(bf16[512,1024]{1,0:T(8,128)(2,1)S(1)} %get-tuple-element.47.xn_ref) | copy-start | bytes 3145732
  48.0 73.7 %copy-start.9 = (f32[512,128]{1,0:T(8,128)}, f32[512,128]{1,0:T(8,128)S(1)}, u32[]{:S(2)}) copy-start(f32[512,128]{1,0:T(8,128)S(1)} %get-tuple-element.50.dbc_ref) | copy-start | bytes 786436
  48.1 73.6 %copy-start.8 = (f32[16,2048]{1,0:T(8,128)}, f32[16,2048]{1,0:T(8,128)S(1)}, u32[]{:S(2)}) copy-start(f32[16,2048]{1,0:T(8,128)S(1)} %broadcast_multiply_fusion.rate_ref.rate2_ref) | copy-start | bytes 393220
  48.2 73.5 %copy-start.4 = (bf16[4,16,8,512]{3,2,0,1:T(8,128)(2,1)}, bf16[4,16,8,512]{3,2,0,1:T(8,128)(2,1)S(1)}, u32[]{:S(2)}) copy-start(bf16[4,16,8,512]{3,2,0,1:T(8,128)(2,1)S(1)} %copy.50) | copy-start | bytes 1572868
  49.0 1.6 copy-start
  216.1 20.0 %copy-start.16 = (f32[16,2048]{1,0:T(8,128)S(1)}, f32[16,2048]{1,0:T(8,128)}, u32[]{:S(2)}) copy-start(f32[16,2048]{1,0:T(8,128)} %get-tuple-element.68) | copy-start | bytes 393220
  216.1 22.7 %copy-start.20 = (f32[1,2048]{1,0:T(1,128)S(1)}, f32[1,2048]{1,0:T(1,128)}, u32[]{:S(2)}) copy-start(f32[1,2048]{1,0:T(1,128)} %get-tuple-element.71) | copy-start | bytes 24580
  216.1 22.7 %copy-start.19 = (f32[1,2048]{1,0:T(1,128)S(1)}, f32[1,2048]{1,0:T(1,128)}, u32[]{:S(2)}) copy-start(f32[1,2048]{1,0:T(1,128)} %get-tuple-element.72) | copy-start | bytes 24580
  239.1 59.3 %copy-start.14 = (bf16[2,2,2,32,2048]{4,3,2,1,0:T(8,128)(2,1)S(1)}, bf16[2,2,2,32,2048]{4,3,2,1,0:T(8,128)(2,1)}, u32[]{:S(2)}) copy-start(bf16[2,2,2,32,2048]{4,3,2,1,0:T(8,128)(2,1)} %get-tuple-element.76) | copy-start | bytes 3145732
  298.4 3.9 %copy-start.15 = (bf16[2,2,2,32,512]{4,3,2,1,0:T(8,128)(2,1)S(1)}, bf16[2,2,2,32,512]{4,3,2,1,0:T(8,128)(2,1)}, u32[]{:S(2)}) copy-start(bf16[2,2,2,32,512]{4,3,2,1,0:T(8,128)(2,1)} %get-tuple-element.74) | copy-start | bytes 786436
  298.4 7.7 %copy-start.13 = (bf16[2,2,2,64,1024]{4,3,2,1,0:T(8,128)(2,1)S(1)}, bf16[2,2,2,64,1024]{4,3,2,1,0:T(8,128)(2,1)}, u32[]{:S(2)}) copy-start(bf16[2,2,2,64,1024]{4,3,2,1,0:T(8,128)(2,1)} %get-tuple-element.77) | copy-start | bytes 3145732
where the time goes:
time: 309 us; the launch traced here: 308 us
  Pallas kernels  276 us (89%)
  local copies, waits for them, and re-layouts  20 us (6%)
  other arithmetic  10.1 us (3%)
    pallas_call x1, Pallas kernels, scan_backward(): pl.pallas_call(functools.partial(backward_kernel, rank, count), grid=(ste...  93.7 us
    pallas_call x1, Pallas kernels, reduce_gradients(): pl.pallas_call(functools.partial(reduce_kernel, count), out_shape=[jax.Sh...  58 us
    pallas_call x1, Pallas kernels, scan_forward(): pl.pallas_call(functools.partial(forward_kernel, rank, group, count), gri...  43.7 us
    pallas_call x1, Pallas kernels, middle(): pl.pallas_call(middle_kernel, grid=(width // block,), in_specs=[whole_spe...  27.3 us
    pallas_call x1, Pallas kernels, gather_weights(): pl.pallas_call(functools.partial(gather_kernel, count), out_shape=[gather...  23.3 us
    pallas_call x1, Pallas kernels, tail(): pl.pallas_call(tail_kernel, grid=(width // block,), in_specs=[channels, w...  18.8 us
    pallas_call x1, Pallas kernels, front(): pl.pallas_call(front_kernel, grid=(width // block,), in_specs=[whole_spec...  11.5 us

commit v1 on v0

--- a/solution.py
+++ b/solution.py
@@ -10,10 +10,13 @@
 QLEN = 16
 LANES = 128
 WIDE = 256
+SPREAD_TIMES = (4, 7, 11)
+INNER_TIMES = (0, 1, 4, 6, 7, 8, 9, 10, 12)
+SMALL_TIMES = (0, 1, 3, 4, 5, 6, 7, 8, 9)
 NEVER = 1e30
 LOG2E = 1.4426950408889634
-FORWARD_STEPS = (0, 2, 3, 4, 5, 6)
-BACKWARD_STEPS = (0, 3, 7, 10, 12, 14, 15)
+FORWARD_STEPS = (0, 4, 7, 9, 12, 14)
+BACKWARD_TIMES = (0, 3, 8, 11, 13, 16)
 
 
 EPSILON = 1e-05
@@ -255,8 +258,15 @@
 
 
 DIMS = ("pair", "high", "low", "bit")
-HALVE = (("pair", "bit", "low", "high"), ("bit", "low", "pair", "high"), ("low", "pair", "bit", "high"))
-SPREAD = (("high", "bit", "low"), ("high", "low", "bit"), ("high", "bit", "low"))
+PARTS = 4
+MIXED = (
+    ("pair", "bit", "low", "high"),
+    ("bit", "low", "pair", "high"),
+    ("low", "pair", "bit", "high"),
+    ("pair", "low", "bit", "high"),
+)
+PAIR_FIRST = (("pair", "bit", "low", "high"), ("pair", "low", "bit", "high")) * 2
+SPREAD = (("high", "low", "bit"), ("high", "bit", "low"), ("high", "low", "bit"), ("high", "low", "bit"))
 EVERY = slice(None)
 
 
@@ -272,165 +282,142 @@
     lax.fori_loop(0, 2**free, step, 0)
 
 
-def cut_parts(shape):
-    axis, tile = (1, 128) if shape[1] >= 512 else (0, 16)
-    tiles = shape[axis] // tile
-    sizes = [(tiles + 2 - k) // 3 * tile for k in range(3)]
-    return [(axis, sum(sizes[:k]), sizes[k]) for k in range(3)]
-
-
-class Reduction:
-    def __init__(self, grads, outs, scratch):
-        count = len(grads)
-        self.grads, self.outs = grads, outs
-        self.accs, self.cores, self.fulls = (scratch[i * count : (i + 1) * count] for i in range(3))
-        rest = scratch[3 * count :]
-        self.arrived = [[[rest[(s * count + a) * 3 + k] for k in range(3)] for a in range(count)] for s in range(4)]
-        self.load_sem, self.core_sem, self.half_sem, self.full_sem, self.out_sem = rest[12 * count :]
-        self.parts = [cut_parts(g.shape[4:]) for g in grads]
-        self.jobs = [(k, a) for k in range(3) for a in range(count)]
-        self.own = own_bits()
-        self.link = Link(self.own)
-        self.stages = [self.begin, self.join, *(functools.partial(self.halved, s) for s in range(4))]
-        self.stages += [*(functools.partial(self.spread, s) for s in range(3)), self.end]
-
-    def part(self, k, a):
-        axis, start, size = self.parts[a][k]
-        return (pl.ds(start, size), EVERY) if axis == 0 else (EVERY, pl.ds(start, size))
-
-    def region(self, chosen, dims, k, a):
-        return tuple(chosen.get(d, EVERY) for d in dims) + self.part(k, a)
-
-    def loading(self, k, a, y):
-        at = self.region({"pair": y}, DIMS, k, a)
+def part_columns(columns, k):
+    return pl.ds(k * (columns // PARTS), columns // PARTS)
+
+
+def region(chosen, dims, columns, k):
+    return tuple(chosen.get(d, EVERY) for d in dims) + (EVERY, part_columns(columns, k))
+
+
+class Halving:
+    def __init__(self, link, orders, local, scratch, given=None):
+        self.link, self.own, self.orders, self.local, self.given = link, link.own, orders, local, given
+        self.cores, *self.arrived, self.load_sem, self.core_sem, self.half_sem = scratch
+        self.columns = local.shape[-1]
+
+    def lead(self, core):
+        return () if self.given is not None else (core,)
+
+    def of_pair(self, y, k):
+        return region({"pair": y}, DIMS, self.columns, k)
+
+    def loading(self, k, y):
+        at = self.of_pair(y, k)
         kept = (2 * y + self.own["core"],) + at[1:]
-        return pltpu.make_async_copy(self.grads[a].at[kept], self.accs[a].at[at], self.load_sem.at[a, k, y])
-
-    def begin(self):
-        greet(self.own, ("core", "pair", "bit", "low", "high"))
-        for k, a in self.jobs:
-            for y in range(2):
-                self.link.send(functools.partial(self.given, k, a, y))
-                self.loading(k, a, y).start()
-
-    def given(self, k, a, y):
-        at = self.region({"pair": y}, DIMS, k, a)
-        other = (2 * y + 1 - self.own["core"],) + at[1:]
-        sems = (self.core_sem.at[0, a, k, y], self.core_sem.at[1, a, k, y])
-        return self.grads[a].at[other], self.cores[a].at[at], sems, "core"
-
-    def half(self, k, a, step):
-        dim = HALVE[k][step]
-        chosen = {d: self.own[d] for d in HALVE[k][:step]}
+        return pltpu.make_async_copy(self.given.at[kept], self.local.at[at], self.load_sem.at[k, y])
+
+    def giving(self, k, y):
+        at = self.of_pair(y, k)
+        other = 1 - self.own["core"]
+        if self.given is not None:
+            src = self.given.at[(2 * y + other,) + at[1:]]
+        else:
+            src = self.local.at[(other,) + at]
+        return src, self.cores.at[at], (self.core_sem.at[0, k, y], self.core_sem.at[1, k, y]), "core"
+
+    def give(self, k):
+        for y in range(2):
+            self.link.send(functools.partial(self.giving, k, y))
+            if self.given is not None:
+                self.loading(k, y).start()
+
+    def join(self, k):
+        for y in range(2):
+            if self.given is not None:
+                self.loading(k, y).wait()
+            sems = (self.core_sem.at[0, k, y], self.core_sem.at[1, k, y])
+            self.link.receive(self.cores.at[self.of_pair(y, k)], sems, "core")
+
+        def add(index):
+            at = index + (EVERY, part_columns(self.columns, k))
+            kept = self.lead(self.own["core"]) + at
+            self.local[kept] = self.local[kept] + self.cores[at]
+
+        each_block(4, add)
+        self.halve(k, 0)
+
+    def half(self, k, step):
+        dim = self.orders[k][step]
+        chosen = {d: self.own[d] for d in self.orders[k][:step]}
         chosen[dim] = 1 - self.own[dim]
-        sems = (self.half_sem.at[0, a, k, step], self.half_sem.at[1, a, k, step])
-        return self.accs[a].at[self.region(chosen, DIMS, k, a)], self.arrived[step][a][k], sems, dim
-
-    def halve(self, k, a, step):
-        self.link.send(functools.partial(self.half, k, a, step))
-
-    def join(self):
-        for k, a in self.jobs:
-            for y in range(2):
-                self.loading(k, a, y).wait()
-                sems = (self.core_sem.at[0, a, k, y], self.core_sem.at[1, a, k, y])
-                self.link.receive(self.cores[a].at[self.region({"pair": y}, DIMS, k, a)], sems, "core")
-
-            def add(lead):
-                at = lead + self.part(k, a)
-                self.accs[a][at] = self.accs[a][at] + self.cores[a][at]
-
-            each_block(4, add)
-            self.halve(k, a, 0)
-
-    def halved(self, step):
-        for k, a in self.jobs:
-            sems = (self.half_sem.at[0, a, k, step], self.half_sem.at[1, a, k, step])
-            self.link.receive(self.arrived[step][a][k], sems, HALVE[k][step])
-            chosen = {d: self.own[d] for d in HALVE[k][: step + 1]}
-            free = [d for d in DIMS if d not in chosen]
-
-            def add(lead):
-                at = tuple(chosen[d] if d in chosen else lead[free.index(d)] for d in DIMS) + self.part(k, a)
-                total = self.accs[a][at] + self.arrived[step][a][k][lead + (EVERY, EVERY)]
-                if step < 3:
-                    self.accs[a][at] = total
-                else:
-                    self.fulls[a][at[1:]] = total
-
-            each_block(len(free), add)
+        at = self.lead(self.own["core"]) + region(chosen, DIMS, self.columns, k)
+        sems = (self.half_sem.at[0, k, step], self.half_sem.at[1, k, step])
+        return self.local.at[at], self.arrived[step].at[k], sems, dim
+
+    def halve(self, k, step):
+        self.link.send(functools.partial(self.half, k, step))
+
+    def halved(self, k, step, done=None):
+        sems = (self.half_sem.at[0, k, step], self.half_sem.at[1, k, step])
+        self.link.receive(self.arrived[step].at[k], sems, self.orders[k][step])
+        chosen = {d: self.own[d] for d in self.orders[k][: step + 1]}
+        free = [d for d in DIMS if d not in chosen]
+
+        def add(index):
+            at = tuple(chosen[d] if d in chosen else index[free.index(d)] for d in DIMS)
+            kept = self.lead(self.own["core"]) + at + (EVERY, part_columns(self.columns, k))
+            total = self.local[kept] + self.arrived[step][(k,) + index + (EVERY, EVERY)]
             if step < 3:
-                self.halve(k, a, step + 1)
+                self.local[kept] = total
             else:
-                self.pass_on(k, a, 0)
-
-    def held(self, k, a, step):
-        chosen = {d: self.own[d] for d in SPREAD[k][step:]}
-        here = self.fulls[a].at[self.region(chosen, DIMS[1:], k, a)]
-        return here, here, (self.full_sem.at[0, a, k, step], self.full_sem.at[1, a, k, step]), SPREAD[k][step]
-
-    def pass_on(self, k, a, step):
-        self.link.send(functools.partial(self.held, k, a, step))
-
-    def spread(self, step):
-        for k, a in self.jobs:
-            chosen = {d: self.own[d] for d in SPREAD[k][step:]}
-            dim = SPREAD[k][step]
-            chosen[dim] = 1 - self.own[dim]
-            there = self.fulls[a].at[self.region(chosen, DIMS[1:], k, a)]
-            self.link.receive(there, (self.full_sem.at[0, a, k, step], self.full_sem.at[1, a, k, step]), dim)
-            if step < 2:
-                self.pass_on(k, a, step + 1)
-
-    def end(self):
-        stores = [
-            pltpu.make_async_copy(self.fulls[a], self.outs[a], self.out_sem.at[a]) for a in range(len(self.outs))
-        ]
-        for copy in stores:
-            copy.start()
-        for copy in stores:
-            copy.wait()
-        self.link.finish()
+                done(k, total)
+
+        each_block(len(free), add)
+        if step < 3:
+            self.halve(k, step + 1)
 
     @staticmethod
-    def scratch(grads):
-        count = len(grads)
+    def scratch(rows, columns):
         dma = pltpu.SemaphoreType.DMA
         low = jnp.bfloat16
-        shapes = [pltpu.VMEM((2, 2, 2, 2) + g.shape[4:], low) for g in grads] * 2
-        shapes += [pltpu.VMEM((2, 2, 2) + g.shape[4:], low) for g in grads]
-        for step in range(4):
-            for g in grads:
-                for axis, _, size in cut_parts(g.shape[4:]):
-                    block = (size, g.shape[5]) if axis == 0 else (g.shape[4], size)
-                    shapes.append(pltpu.VMEM((2,) * (3 - step) + block, low))
-        return shapes + [
-            dma((count, 3, 2)),
-            dma((2, count, 3, 2)),
-            dma((2, count, 3, 4)),
-            dma((2, count, 3, 3)),
-            dma((count,)),
-        ]
-
-
-def reduce_kernel(count, *refs):
-    for stage in Reduction(refs[:count], refs[count : 2 * count], refs[2 * count :]).stages:
-        stage()
-
-
-def reduce_gradients(grads, collective_id):
-    count = len(grads)
-    return pl.pallas_call(
-        functools.partial(reduce_kernel, count),
-        out_shape=[jax.ShapeDtypeStruct(g.shape[1:], g.dtype) for g in grads],
-        in_specs=[pl.BlockSpec(memory_space=pl.ANY)] * count,
-        out_specs=[pl.BlockSpec(memory_space=pl.ANY)] * count,
-        scratch_shapes=Reduction.scratch(grads),
-        compiler_params=pltpu.CompilerParams(
-            collective_id=collective_id, has_side_effects=True, vmem_limit_bytes=56 << 20
-        ),
-        name="reduce_gradients",
-    )(*grads)
+        shapes = [pltpu.VMEM((2, 2, 2, 2, rows, columns), low)]
+        shapes += [pltpu.VMEM((PARTS,) + (2,) * (3 - step) + (rows, columns // PARTS), low) for step in range(4)]
+        return shapes + [dma((PARTS, 2)), dma((2, PARTS, 2)), dma((2, PARTS, 4))]
+
+
+class Spreading:
+    def __init__(self, link, full, sems):
+        self.link, self.own, self.full, self.sems = link, link.own, full, sems
+        self.columns = full.shape[-1]
+
+    def put(self, k, value):
+        at = tuple(self.own[d] for d in DIMS[1:]) + (EVERY, part_columns(self.columns, k))
+        self.full[at] = value
+        self.pass_on(k, 0)
+
+    def held(self, k, step):
+        chosen = {d: self.own[d] for d in SPREAD[k][step:]}
+        here = self.full.at[region(chosen, DIMS[1:], self.columns, k)]
+        return here, here, (self.sems.at[0, k, step], self.sems.at[1, k, step]), SPREAD[k][step]
+
+    def pass_on(self, k, step):
+        self.link.send(functools.partial(self.held, k, step))
+
+    def take(self, k, step):
+        dim = SPREAD[k][step]
+        chosen = {d: self.own[d] for d in SPREAD[k][step:]}
+        chosen[dim] = 1 - self.own[dim]
+        there = self.full.at[region(chosen, DIMS[1:], self.columns, k)]
+        self.link.receive(there, (self.sems.at[0, k, step], self.sems.at[1, k, step]), dim)
+        if step < 2:
+            self.pass_on(k, step + 1)
+
+    @staticmethod
+    def scratch(rows, columns):
+        return [pltpu.VMEM((2, 2, 2, rows, columns), jnp.bfloat16), pltpu.SemaphoreType.DMA((2, PARTS, 3))]
+
+
+def run_events(events, last):
+    events = sorted(events, key=lambda event: event[0])
+    for step in range(last + 1):
+        actions = [action for time, action in events if min(int(time), last) == step]
+        if actions:
+
+            @pl.when(pl.program_id(0) == step)
+            def _():
+                for action in actions:
+                    action()
 
 
 def block_rows(values, row, rows):
@@ -451,7 +438,7 @@
 
 
 TAPS = 4
-BIAS_ROW, STEP_ROW, SKIP_ROW = 4, 5, 6
+BIAS_ROW, STEP_ROW, SKIP_ROW, GAIN_ROW = 4, 5, 6, 7
 
 
 def front_kernel(tokens_ref, gain_ref, w_ref, rows_ref, xproj_ref, mask_ref, inner_ref, pre_ref, u_ref, dbc_ref, xn_ref, xnt_ref):
@@ -489,7 +476,7 @@
     return pl.BlockSpec((block, columns), lambda i: (i, 0))
 
 
-def front(tokens, gain, inner_w, by_channel, xproj_t, masks, block=256):
+def front(tokens, gain, inner_w, by_channel, xproj_t, masks, block=512):
     length, features = tokens.shape
     width = inner_w.shape[1]
     low, wide = jnp.bfloat16, jnp.float32
@@ -678,7 +665,7 @@
         mixed_ref[...] = (tokens_ref[...].astype(jnp.float32) + live * branch[...]).astype(mixed_ref.dtype)
 
 
-def middle(xn, xnt, gate_w, y, u, by_channel, out_w, cotangent, tokens, masks, block=256):
+def middle(xn, xnt, gate_w, y, u, by_channel, out_w, cotangent, tokens, masks, block=512):
     length, features = tokens.shape
     width = gate_w.shape[1]
     low, wide = jnp.bfloat16, jnp.float32
@@ -722,17 +709,35 @@
     )(xn, xnt, gate_w, y, u, by_channel, out_w, cotangent, tokens, masks)
 
 
-def backward_kernel(rank, count, u_ref, dt_ref, dy_ref, dbc_ref, mask_ref, h_ref, before_ref, rows_ref, dtproj_ref, rate2_ref, rate_ref, *refs):
+def backward_kernel(rank, count, steps, u_ref, dt_ref, dy_ref, dbc_ref, mask_ref, h_ref, before_ref, rows_ref, dtproj_ref, rate2_ref, rate_ref, *refs):
     grads, (du_ref, ddbc_ref, ldt_ref, dtproj_grad, bias_grad) = refs[:count], refs[count : count + 5]
-    outs, refs = refs[count + 5 : 2 * count + 5], refs[2 * count + 5 :]
+    sums, refs = refs[count + 5 : 2 * count + 5], refs[2 * count + 5 :]
     message, long_s, feed_s, c_s, bblk_s, g_s, lrate_s, db_s, dc_s, before_s, e_s, lsum_s, small_s = refs[:13]
     blocks, _, width = dt_ref.shape
     states = rate_ref.shape[0]
     span = QLEN * states
     low, wide = jnp.bfloat16, jnp.float32
-    reduction = Reduction(grads, outs, refs[13:])
-    early = len(BACKWARD_STEPS)
-    run_stages(reduction.stages[:early], BACKWARD_STEPS)
+    link = Link(own_bits())
+    per = (len(refs) - 13) // count
+    halvings = []
+    for a in range(count):
+        local, *scratch = refs[13 + a * per : 13 + (a + 1) * per]
+        halvings.append(Halving(link, MIXED, local, scratch, given=grads[a]))
+
+    def keep_sum(out, k, total):
+        out[:, part_columns(out.shape[1], k)] = total
+
+    events = [(0, lambda: greet(link.own, ("core", "pair", "bit", "low", "high")))]
+    for k in range(PARTS):
+        for halving, out in zip(halvings, sums):
+            give, join, *times = BACKWARD_TIMES
+            events += [(give, functools.partial(halving.give, k)), (join, functools.partial(halving.join, k))]
+            events += [
+                (time, functools.partial(halving.halved, k, step, functools.partial(keep_sum, out)))
+                for step, time in enumerate(times)
+            ]
+    final = steps - 1
+    run_events([event for event in events if event[0] <= final], final)
 
     @pl.when(pl.program_id(0) == 0)
     def _():
@@ -827,8 +832,7 @@
         d_rank += transposed_product(d_step, dtproj_ref[:, s])
         du_ref[:, s] = d_y * rows_ref[SKIP_ROW : SKIP_ROW + 1, s] + e * dt
     ddbc_ref[...] = (jnp.where(lane_index(d_rank.shape) < rank, d_rank, 0.0) + small_s[...]).astype(low)
-    late = reduction.stages[early:]
-    run_stages(late, (pl.num_programs(0) - 1,) * len(late))
+    run_events([event for event in events if event[0] > final] + [(steps, link.finish)], final)
 
 
 def scan_backward(rank, u, dt, d_y, dbc, masks, h, by_channel, dtproj, rate2, rate, grads, collective_id, blocks=2):
@@ -844,7 +848,7 @@
     cubes = pl.BlockSpec((blocks, QLEN, width), lambda i: (steps - 1 - i, 0, 0))
     in_blocks = lambda v: v.reshape(tokens // QLEN, QLEN, width)
     du, ddbc, ldt, dtproj_grad, bias_grad, *sums = pl.pallas_call(
-        functools.partial(backward_kernel, rank, count),
+        functools.partial(backward_kernel, rank, count, steps),
         grid=(steps,),
         in_specs=[
             flat(width),
@@ -866,7 +870,7 @@
             whole_spec(rate2.shape),
             whole_spec(dtproj.shape),
             whole_spec((1, width)),
-            *anywhere,
+            *(whole_spec(g.shape[4:]) for g in grads),
         ],
         out_shape=[
             jax.ShapeDtypeStruct((tokens, width), wide),
@@ -874,7 +878,7 @@
             jax.ShapeDtypeStruct(rate2.shape, wide),
             jax.ShapeDtypeStruct(dtproj.shape, wide),
             jax.ShapeDtypeStruct((1, width), wide),
-            *(jax.ShapeDtypeStruct(g.shape[1:], g.dtype) for g in grads),
+            *(jax.ShapeDtypeStruct(g.shape[4:], g.dtype) for g in grads),
         ],
         scratch_shapes=[
             pltpu.VMEM((states, width), wide),
@@ -890,7 +894,11 @@
             pltpu.VMEM((rows, width), wide),
             pltpu.VMEM((rows, width), wide),
             pltpu.VMEM((rows, LANES), wide),
-            *Reduction.scratch(grads),
+            *(
+                shape
+                for g in grads
+                for shape in (pltpu.VMEM((2, 2, 2, 2) + g.shape[4:], low), *Halving.scratch(*g.shape[4:]))
+            ),
         ],
         compiler_params=pltpu.CompilerParams(
             collective_id=collective_id, has_side_effects=True, vmem_limit_bytes=56 << 20
@@ -901,12 +909,49 @@
 
 
 def tail_kernel(
-    du_ref, ddbc_ref, xproj_ref, u_ref, inner_ref, pre_ref, rows_ref, mask_ref, xnt_ref, w_ref, dgate_ref, tokens_ref, cot_ref, gain_ref,
-    innergrad_ref, xprojgrad_ref, rowgrad_ref, tokengrad_ref, gaingrad_ref, dxn
+    steps, rank, count, du_ref, ddbc_ref, xproj_ref, u_ref, inner_ref, pre_ref, rows_ref, mask_ref, xnt_ref, w_ref, dgate_ref, tokens_ref, cot_ref, gain_ref,
+    dtproj_ref, alog_ref, bias_ref, skip_ref, *refs
 ):
-    wide = jnp.float32
-
-    @pl.when(pl.program_id(0) == 0)
+    wide, low = jnp.float32, jnp.bfloat16
+    pieces, tokengrad_ref, outs = refs[:count], refs[count], refs[count + 1 : 2 * count + 3]
+    refs = refs[2 * count + 3 :]
+    dxn, xproj_s, row_s, inner_s, small_s, out_sem = refs[:6]
+    link = Link(own_bits())
+    halving_refs, spreading_refs = refs[6 : 6 + 16], refs[6 + 16 :]
+    spreadings = [Spreading(link, *spreading_refs[2 * a : 2 * a + 2]) for a in range(count + 2)]
+    inner_sum = Halving(link, PAIR_FIRST, inner_s, halving_refs[:8])
+    small_sum = Halving(link, PAIR_FIRST, small_s, halving_refs[8:])
+    block = du_ref.shape[1]
+    here = pl.program_id(0)
+    columns = pl.ds(pl.multiple_of(here * block, block), block)
+    final = steps - 1
+
+    def start():
+        greet(link.own, ("core", "pair", "bit", "low", "high"))
+        for k in range(PARTS):
+            for piece, spreading in zip(pieces, spreadings):
+                spreading.put(k, piece[:, part_columns(piece.shape[1], k)])
+
+    def add_up(events, halving, spreading, k, first, times):
+        give, join, *halves = times[:6]
+        events += [(first + give, functools.partial(halving.give, k)), (first + join, functools.partial(halving.join, k))]
+        events += [
+            (first + time, functools.partial(halving.halved, k, step, spreading.put)) for step, time in enumerate(halves)
+        ]
+        events += [
+            (first + time, functools.partial(spreading.take, k, step)) for step, time in enumerate(times[6:])
+        ]
+
+    events = []
+    for k in range(PARTS):
+        for spreading in spreadings[:count]:
+            events += [(time, functools.partial(spreading.take, k, step)) for step, time in enumerate(SPREAD_TIMES)]
+        ready = (k + 1) * steps // PARTS - 1
+        add_up(events, inner_sum, spreadings[count], k, ready, INNER_TIMES)
+        add_up(events, small_sum, spreadings[count + 1], k, final, SMALL_TIMES)
+    run_events([(0, start)], final)
+
+    @pl.when(here == 0)
     def _():
         dxn[...] = dgate_ref[...]
 
@@ -926,31 +971,72 @@
         sums[TAPS - 1 - offset] = jnp.sum(back * inner, axis=0, keepdims=True)
         d_inner = d_inner + block_rows(rows, TAPS - 1 - offset, 1) * back
     nothing = jnp.zeros_like(sums[0])
-    rowgrad_ref[...] = jnp.concatenate([nothing if v is None else v for v in sums], axis=0)
-    xprojgrad_ref[...] = rows_product(ddbc_ref[...], u_ref[...])
-    d_inner = d_inner.astype(jnp.bfloat16)
-    innergrad_ref[...] = dot(xnt_ref[...], d_inner).astype(innergrad_ref.dtype)
+    row_s[:, columns] = jnp.concatenate([nothing if v is None else v for v in sums], axis=0)
+    xproj_s[:, columns] = rows_product(ddbc_ref[...], u_ref[...])
+    d_inner = d_inner.astype(low)
+    inner_grad = dot(xnt_ref[...], d_inner).astype(low)
+    size = inner_grad.shape[0] // 4
+    for shard in range(4):
+        own_rows = inner_grad[shard * size : (shard + 1) * size]
+        inner_s[shard % 2, shard // 2, :, :, :, :, columns] = own_rows.reshape(2, 2, 2, size // 8, block)
     dxn[...] += transposed_product(d_inner, w_ref[...])
 
-    @pl.when(pl.program_id(0) == pl.num_programs(0) - 1)
+    @pl.when(here == final)
     def _():
         x = tokens_ref[...].astype(wide)
         inv = lax.rsqrt(jnp.mean(x * x, axis=1, keepdims=True) + EPSILON)
         x_hat = x * inv
-        gaingrad_ref[...] = jnp.sum(dxn[...] * x_hat, axis=0, keepdims=True)
+        gain_grad = jnp.sum(dxn[...] * x_hat, axis=0, keepdims=True)
         d_hat = dxn[...] * gain_ref[...]
         level = jnp.mean(d_hat * x_hat, axis=1, keepdims=True)
         tokengrad_ref[...] = cot_ref[...].astype(wide) + inv * (d_hat - x_hat * level)
-
-
-def tail(du, ddbc, xproj_t, u, inner, pre, by_channel, masks, xnt, inner_w, dxn_gate, tokens, cotangent, gain, block=256):
+        owned = xproj_s.shape[1] // 4
+        states = alog_ref.shape[0]
+        part = gain_grad.shape[1] // 4
+        row = lax.broadcasted_iota(jnp.int32, (8, owned), 0)
+        for shard in range(4):
+            own = slice(shard * owned, (shard + 1) * owned)
+            gains = jnp.concatenate(
+                [gain_grad[:, shard * part : (shard + 1) * part], jnp.zeros((1, owned - part), wide)], axis=1
+            )
+            rows = row_s[:, own]
+            for at, extra in ((STEP_ROW, bias_ref[:, own]), (SKIP_ROW, skip_ref[:, own]), (GAIN_ROW, gains)):
+                rows = jnp.where(row == at, extra, rows)
+            stacked = [dtproj_ref[:rank, own], alog_ref[:, own], xproj_s[: rank + 2 * states, own], rows]
+            height = 8 * small_s.shape[5]
+            stacked.append(jnp.zeros((height - sum(v.shape[0] for v in stacked), owned), wide))
+            stacked = jnp.concatenate(stacked, axis=0).astype(low)
+            small_s[shard % 2, shard // 2] = stacked.reshape(2, 2, 2, height // 8, owned)
+
+    run_events(events, final)
+
+    @pl.when(here == final)
+    def _():
+        stores = [pltpu.make_async_copy(s.full, o, out_sem.at[i]) for i, (s, o) in enumerate(zip(spreadings, outs))]
+        for copy in stores:
+            copy.start()
+        for copy in stores:
+            copy.wait()
+        link.finish()
+
+
+def tail(
+    rank, du, ddbc, xproj_t, u, inner, pre, by_channel, masks, xnt, inner_w, dxn_gate, tokens, cotangent, gain,
+    dtproj_grad, alog_grad, bias_grad, skip_grad, pieces, collective_id, block=256,
+):
     length, features = tokens.shape
     width = inner_w.shape[1]
+    count = len(pieces)
+    steps = width // block
+    inner_shape = (features // 32, width)
+    used = 2 * rank + 3 * alog_grad.shape[0] + 8
+    small_shape = ((used + -used % LANES) // 8, width // 4)
+    shapes = [*(p.shape for p in pieces), inner_shape, small_shape]
     low, wide = jnp.bfloat16, jnp.float32
     channels = columns_spec(length, block)
-    return pl.pallas_call(
-        tail_kernel,
-        grid=(width // block,),
+    token_grad, *sums = pl.pallas_call(
+        functools.partial(tail_kernel, steps, rank, count),
+        grid=(steps,),
         in_specs=[
             channels,
             whole_spec(ddbc.shape),
@@ -966,25 +1052,37 @@
             whole_spec(tokens.shape),
             whole_spec(tokens.shape),
             whole_spec(gain.shape),
-        ],
-        out_specs=[
-            columns_spec(features, block),
-            columns_spec(LANES, block),
-            columns_spec(8, block),
-            whole_spec(tokens.shape),
-            whole_spec((1, features)),
-        ],
+            whole_spec(dtproj_grad.shape),
+            whole_spec(alog_grad.shape),
+            whole_spec(bias_grad.shape),
+            whole_spec(skip_grad.shape),
+            *(whole_spec(p.shape) for p in pieces),
+        ],
+        out_specs=[whole_spec(tokens.shape), *[pl.BlockSpec(memory_space=pl.ANY)] * (count + 2)],
         out_shape=[
-            jax.ShapeDtypeStruct((features, width), low),
-            jax.ShapeDtypeStruct((LANES, width), wide),
-            jax.ShapeDtypeStruct((8, width), wide),
             jax.ShapeDtypeStruct(tokens.shape, wide),
-            jax.ShapeDtypeStruct((1, features), wide),
-        ],
-        scratch_shapes=[pltpu.VMEM(tokens.shape, wide)],
-        compiler_params=pltpu.CompilerParams(vmem_limit_bytes=56 << 20),
+            *(jax.ShapeDtypeStruct((2, 2, 2) + shape, low) for shape in shapes),
+        ],
+        scratch_shapes=[
+            pltpu.VMEM(tokens.shape, wide),
+            pltpu.VMEM((LANES, width), wide),
+            pltpu.VMEM((8, width), wide),
+            pltpu.VMEM((2, 2, 2, 2, 2) + inner_shape, low),
+            pltpu.VMEM((2, 2, 2, 2, 2) + small_shape, low),
+            pltpu.SemaphoreType.DMA((count + 2,)),
+            *Halving.scratch(*inner_shape),
+            *Halving.scratch(*small_shape),
+            *(shape for s in shapes for shape in Spreading.scratch(*s)),
+        ],
+        compiler_params=pltpu.CompilerParams(
+            collective_id=collective_id, has_side_effects=True, vmem_limit_bytes=58 << 20
+        ),
         name="tail",
-    )(du, ddbc, xproj_t, u, inner, pre, by_channel, masks, xnt, inner_w, dxn_gate, tokens, cotangent, gain)
+    )(
+        du, ddbc, xproj_t, u, inner, pre, by_channel, masks, xnt, inner_w, dxn_gate, tokens, cotangent, gain,
+        dtproj_grad, alog_grad, bias_grad, skip_grad, *pieces,
+    )
+    return token_grad, sums
 
 
 def add_groups(sums):
@@ -1043,7 +1141,7 @@
         xn, xnt, gate_w, y, u, by_channel, out_full, cotangent, tokens, masks
     )
     in_pieces = lambda v: v.reshape((4, 2, 2, 2, v.shape[0] // 32, v.shape[1]))
-    du, ddbc, ldt, dtproj_local, dtb_local, early_sums = scan_backward(
+    du, ddbc, ldt, dtproj_local, dtb_local, early_pieces = scan_backward(
         rank,
         u,
         dt,
@@ -1058,27 +1156,31 @@
         [in_pieces(gate_local), in_pieces(out_local)],
         3,
     )
-    inner_local, xproj_local, row_local, token_grad, gain_local = tail(
-        du, ddbc, xproj_t, u, inner, pre, by_channel, masks, xnt, inner_w, dxn_gate, tokens, cotangent, gain
+    token_grad, sums = tail(
+        rank,
+        du,
+        ddbc,
+        xproj_t,
+        u,
+        inner,
+        pre,
+        by_channel,
+        masks,
+        xnt,
+        inner_w,
+        dxn_gate,
+        tokens,
+        cotangent,
+        gain,
+        dtproj_local,
+        ldt * decay_rate,
+        dtb_local,
+        skip_local,
+        early_pieces,
+        4,
     )
-    small_local = jnp.concatenate(
-        [
-            dtproj_local[:rank],
-            ldt * decay_rate,
-            xproj_local[: xproj_w.shape[1]],
-            row_local[: TAPS + 1],
-            dtb_local,
-            skip_local,
-            fill(gain_local.reshape(4, -1)).reshape(1, -1),
-        ],
-        axis=0,
-    ).astype(jnp.bfloat16)
-    small_local = jnp.pad(small_local, ((0, -used % LANES), (0, 0)))
-    small_local = jnp.swapaxes(small_local.reshape(small_local.shape[0], 4, owned), 0, 1)
-    small_local = small_local.reshape(4, 2, 2, 2, -1, owned)
-    late_sums = reduce_gradients([in_pieces(inner_local), small_local], 4)
     in_rows = lambda v: v.reshape(-1, v.shape[-1]).astype(jnp.float32)
-    gate_grad, out_grad, inner_grad, small = add_groups([in_rows(v) for v in (*early_sums, *late_sums)])
+    gate_grad, out_grad, inner_grad, small = add_groups([in_rows(v) for v in sums])
     in_grad = jnp.concatenate([inner_grad, gate_grad], axis=1)
     dtproj_grad, alog_grad, xproj_grad = small[:rank], small[rank : rank + states], small[rank + states : used - 8].T
     conv_grad, convb_grad, dtb_grad, skip_grad = small[used - 8 : used - 4], small[used - 4], small[used - 3], small[used - 2]

time: 309 us -> 274 us (0.89)
  Pallas kernels: 276 us -> 244 us
  local copies, waits for them, and re-layouts: 20 us -> 16.7 us
    pallas_call x3 -> x2, Pallas kernels: 171 us -> 152 us  [the longest x1 82.3 us: tail(): pl.pallas_call(functools.partial(tail_kernel, steps, rank, count), grid=(...]
    pallas_call x1, Pallas kernels: 43.7 us -> 35.5 us  [scan_forward(): pl.pallas_call(functools.partial(forward_kernel, rank, group, count), gri...]
    pallas_call x1, Pallas kernels: 27.3 us -> 23.5 us  [middle(): pl.pallas_call(middle_kernel, grid=(width // block,), in_specs=[whole_spe...]
    slice x3 -> x0, local copies, waits for them, and re-layouts: 3.09 us -> none  [the longest x1 1.18 us: body(): xproj_local[:xproj_w.shape[1]]]
where the time goes in v1:
time: 274 us; the launch traced here: 273 us
  Pallas kernels  244 us (89%)
  local copies, waits for them, and re-layouts  16.7 us (6%)
  other arithmetic  11.3 us (4%)
    pallas_call x1, Pallas kernels, tail(): pl.pallas_call(functools.partial(tail_kernel, steps, rank, count), grid=(...  82.3 us
    pallas_call x1, Pallas kernels, scan_backward(): pl.pallas_call(functools.partial(backward_kernel, rank, count, steps), gr...  69.5 us
    pallas_call x1, Pallas kernels, scan_forward(): pl.pallas_call(functools.partial(forward_kernel, rank, group, count), gri...  35.5 us
    pallas_call x1, Pallas kernels, middle(): pl.pallas_call(middle_kernel, grid=(width // block,), in_specs=[whole_spe...  23.5 us
    pallas_call x1, Pallas kernels, gather_weights(): pl.pallas_call(functools.partial(gather_kernel, count), out_shape=[gather...  23.3 us
    pallas_call x1, Pallas kernels, front(): pl.pallas_call(front_kernel, grid=(width // block,), in_specs=[whole_spec...  9.97 us
    unnamed x48, local copies, waits for them, and re-layouts  5.95 us

profile of v1, /device:TPU:0, one launch (start us, length us, event | category | flops | bytes accessed | tf_op | source)
XLA Modules:
  0.0 273.1 jit_solution(8572557125931997101)
XLA Ops:
  0.6 0.0 copy-start.22
  0.7 0.0 copy-start.19
  0.7 0.0 copy-start.20
  0.7 0.0 copy-start.21
  0.7 0.0 copy-start.16
  0.7 0.0 copy-start.18
  0.7 0.0 copy-start.17
  0.7 0.9 reduce-window.4
  1.6 0.7 fusion.3
  2.3 0.7 and_bitcast_fusion
  3.0 0.1 convert_reduce_fusion
  3.0 0.1 fusion.1
  3.1 0.6 slice.71
  3.7 0.7 compare_and_fusion
  4.5 0.2 copy.41
  4.7 0.0 copy-start.2
  4.7 0.0 copy-start.3
  4.7 1.8 fusion.4
  6.5 0.0 copy-done.22
  6.5 0.0 copy-done.19
  6.6 0.0 copy-done.20
  6.6 0.0 copy-done.21
  6.6 0.0 copy-done.16
  6.6 0.0 copy-done.18
  6.6 0.0 copy-done.17
  6.6 3.4 %concatenate.27 = bf16[184,512]{1,0:T(8,128)(2,1)} concatenate(bf16[64,512]{1,0:T(8,128)(2,1)} %param.23, bf16[16,512]{1,0:T(8,128)(2,1)S(1)} %copy-done.17, bf16[96,512]{1,0:T(8,128)(2,1)S(1)} %bitcast.72, bf16[4,512]{1,0:T(4,128)(2,1)S(1)} %copy-done.18, bf16[1,512]{1,0:T(2,128)(2,1)S(1)} %broadcast_in_dim.15, bf16[1,512]{1,0:T(2,128)(2,1)S(1)} %broadcast_in_dim.16, ...), dimensions={0} | concatenate | bytes 376832 | tf_op jit(solution)/shard_map/concatenate | solution.py:1120
  10.0 0.9 pad.11.refs_1_
  10.9 23.3 %gather_weights.1 = (bf16[4,256,2048]{2,1,0:T(8,128)(2,1)S(1)}, bf16[4,256,512]{2,1,0:T(8,128)(2,1)S(1)}) custom-call(bf16[256,2048]{1,0:T(8,128)(2,1)S(1)} %get-tuple-element.75.refs_0_, bf16[256,512]{1,0:T(8,128)(2,1)S(1)} %pad.11.refs_1_), custom_call_target="tpu_custom_call" | custom-call | tf_op jit(solution)/shard_map/gather_weights/pallas_call | solution.py:237
  34.2 0.0 copy-start.1
  34.3 2.0 copy-done.1
  36.3 0.0 copy-start.7
  36.3 0.1 slice_bitcast_fusion
  36.4 0.0 copy-start.5
  36.5 0.0 copy-start.11
  36.5 0.0 copy-start.12
  36.5 0.0 copy-done.3
  36.5 10.0 %front.1 = (bf16[512,2048]{1,0:T(8,128)(2,1)}, f32[512,2048]{1,0:T(8,128)}, bf16[512,2048]{1,0:T(8,128)(2,1)}, f32[512,128]{1,0:T(8,128)S(1)}, bf16[512,1024]{1,...) custom-call(bf16[512,1024]{1,0:T(8,128)(2,1)S(1)} %copy-done.3, f32[1,1024]{1,0:T(1,128)S(1)} %convert.11.gain_ref, ...), custom_call_target="tpu_custom_call" | custom-call | tf_op jit(solution)/shard_map/front/pallas_call | solution.py:483
  46.6 0.0 copy-start.8
  46.6 0.0 copy-start.4
  46.7 0.8 copy-done.6
  47.5 0.0 copy-done.2
  47.5 0.0 copy-done.7
  47.5 0.0 copy-done.11
  47.5 1.6 copy-done
  49.1 35.5 %scan_forward.1 = (f32[512,2048]{1,0:T(8,128)}, bf16[8192,2048]{1,0:T(8,128)(2,1)}, f32[512,2048]{1,0:T(8,128)}, bf16[4,256,2048]{2,1,0:T(8,128)(2,1)}, bf16[4,512,1024]{2,1,0:T(8,128)(2,1)}) custom-call(bf16[512,2048]{1,0:T(8,128)(2,1)S(1)} %copy-done, f32[512,128]{1,0:T(8,128)S(1)} %get-tuple-element.48.dbc_ref, f32[512,4]{1,0:T(8,128)S(1)} %stack.18.mask_ref, ...), custom_call_target="tpu_custom_call" | custom-call | tf_op jit(solution)/shard_map/scan_forward/pallas_call | solution.py:599
  84.6 0.0 copy-done.5
  84.6 0.0 copy-done.12
  84.7 23.5 %middle.1 = (bf16[512,1024]{1,0:T(8,128)(2,1)}, f32[512,2048]{1,0:T(8,128)}, bf16[512,2048]{1,0:T(8,128)(2,1)}, bf16[2048,1024]{1,0:T(8,128)(2,1)}, bf16[1024,20...) custom-call(bf16[512,1024]{1,0:T(8,128)(2,1)} %copy-done.10, bf16[1024,512]{1,0:T(8,128)(2,1)} %copy-done.6, ...), custom_call_target="tpu_custom_call" | custom-call | tf_op jit(solution)/shard_map/middle/pallas_call | solution.py:673
  108.2 0.6 convert_element_type.68.rate_ref
  108.8 69.5 %scan_backward.1 = (f32[512,2048]{1,0:T(8,128)}, bf16[512,128]{1,0:T(8,128)(2,1)}, f32[16,2048]{1,0:T(8,128)}, f32[128,2048]{1,0:T(8,128)}, f32[1,2048]{1,0:T(1,...) custom-call(bf16[512,2048]{1,0:T(8,128)(2,1)} %get-tuple-element.47.u_ref, f32[32,16,2048]{2,1,0:T(8,128)} %bitcast.62, ...), custom_call_target="tpu_custom_call" | custom-call | tf_op jit(solution)/shard_map/scan_backward/pallas_call | solution.py:850
  178.3 1.6 mul.11.alog_ref
  179.9 82.3 %tail.1 = (f32[512,1024]{1,0:T(8,128)}, bf16[2,2,2,32,2048]{4,3,2,1,0:T(8,128)(2,1)}, bf16[2,2,2,64,1024]{4,3,2,1,0:T(8,128)(2,1)}, bf16[2,2,2,32,2048]{4,3,2,1,0:T(8,128)(2,1)}, bf16[2,2,2,32,512]{4,3,2,1,0:T(8,128)(2,1)}) custom-call(f32[512,2048]{1,0:T(8,128)} %get-tuple-element.58.du_ref, bf16[512,128]{1,0:T(8,128)(2,1)} %get-tuple-element.59.ddbc_ref, ...), custom_call_target="tpu_custom_call" | custom-call | tf_op jit(solution)/shard_map/tail/pallas_call | solution.py:1037
  262.2 4.2 %maximum_convert_fusion = f32[256,4096]{1,0:T(8,128)} fusion(bf16[256,2048]{1,0:T(8,128)(2,1)} %bitcast.69, bf16[256,2048]{1,0:T(8,128)(2,1)} %bitcast.70), kind=kLoop, calls=%fused_computation | loop fusion | flops 4194304 | bytes 6291456 | tf_op jit(solution)/shard_map/concatenate | solution.py:1184
  266.4 1.6 bitcast_convert_fusion
  268.0 0.0 copy-done.15
  268.0 0.1 bitcast_convert_fusion.1
  268.1 0.7 slice_bitcast_fusion.2
  268.8 0.7 slice.95
  269.4 0.6 slice.97
  270.1 0.6 slice.92
  270.7 0.6 fusion.5
  271.2 0.6 slice.91
  271.8 0.0 copy-done.13
  271.8 1.3 copy.48
  (30 shorter events, 0.3 us)
Async XLA Ops:
  0.6 5.9 %copy-start.22 = (bf16[256]{0:T(256)(128)(2,1)S(1)}, bf16[256]{0:T(256)(128)(2,1)}, u32[]{:S(2)}) copy-start(bf16[256]{0:T(256)(128)(2,1)} %param.18) | copy-start | bytes 1540
  0.7 5.9 %copy-start.19 = (bf16[512]{0:T(512)(128)(2,1)S(1)}, bf16[512]{0:T(512)(128)(2,1)}, u32[]{:S(2)}) copy-start(bf16[512]{0:T(512)(128)(2,1)} %param.21) | copy-start | bytes 3076
  0.7 5.9 %copy-start.20 = (bf16[512]{0:T(512)(128)(2,1)S(1)}, bf16[512]{0:T(512)(128)(2,1)}, u32[]{:S(2)}) copy-start(bf16[512]{0:T(512)(128)(2,1)} %param.24) | copy-start | bytes 3076
  0.7 5.9 %copy-start.21 = (bf16[512]{0:T(512)(128)(2,1)S(1)}, bf16[512]{0:T(512)(128)(2,1)}, u32[]{:S(2)}) copy-start(bf16[512]{0:T(512)(128)(2,1)} %param.26) | copy-start | bytes 3076
  0.7 5.9 %copy-start.16 = (bf16[512,96]{0,1:T(8,128)(2,1)S(1)}, bf16[512,96]{0,1:T(8,128)(2,1)}, u32[]{:S(2)}) copy-start(bf16[512,96]{0,1:T(8,128)(2,1)} %param.22) | copy-start | bytes 294916
  0.7 5.9 %copy-start.18 = (bf16[4,512]{1,0:T(4,128)(2,1)S(1)}, bf16[4,512]{1,0:T(4,128)(2,1)}, u32[]{:S(2)}) copy-start(bf16[4,512]{1,0:T(4,128)(2,1)} %param.20) | copy-start | bytes 12292
  0.7 5.9 %copy-start.17 = (bf16[16,512]{1,0:T(8,128)(2,1)S(1)}, bf16[16,512]{1,0:T(8,128)(2,1)}, u32[]{:S(2)}) copy-start(bf16[16,512]{1,0:T(8,128)(2,1)} %param.25) | copy-start | bytes 49156
  4.7 42.8 %copy-start.2 = (f32[512,4]{1,0:T(8,128)}, f32[512,4]{1,0:T(8,128)S(1)}, u32[]{:S(2)}) copy-start(f32[512,4]{1,0:T(8,128)S(1)} %stack.18.mask_ref) | copy-start | bytes 24580
  4.7 31.8 %copy-start.3 = (bf16[512,1024]{1,0:T(8,128)(2,1)S(1)}, bf16[512,1024]{1,0:T(8,128)(2,1)}, u32[]{:S(2)}) copy-start(bf16[512,1024]{1,0:T(8,128)(2,1)} %tokens_ref.5) | copy-start | bytes 3145732
  34.2 2.0 copy-start.1
  36.3 11.2 %copy-start.7 = (f32[8,2048]{1,0:T(8,128)}, f32[8,2048]{1,0:T(8,128)S(1)}, u32[]{:S(2)}) copy-start(f32[8,2048]{1,0:T(8,128)S(1)} %convert.10.rows_ref) | copy-start | bytes 196612
  36.4 48.2 %copy-start.5 = (bf16[4,16,8,512]{3,2,0,1:T(8,128)(2,1)}, bf16[4,16,8,512]{3,2,0,1:T(8,128)(2,1)S(1)}, u32[]{:S(2)}) copy-start(bf16[4,16,8,512]{3,2,0,1:T(8,128)(2,1)S(1)} %copy.44) | copy-start | bytes 1572868
  36.5 11.0 %copy-start.11 = (bf16[512,1024]{1,0:T(8,128)(2,1)S(1)}, bf16[512,1024]{1,0:T(8,128)(2,1)}, u32[]{:S(2)}) copy-start(bf16[512,1024]{1,0:T(8,128)(2,1)} %refs_1_.1) | copy-start | bytes 3145732
  36.5 48.2 %copy-start.12 = (f32[1,1024]{1,0:T(1,128)}, f32[1,1024]{1,0:T(1,128)S(1)}, u32[]{:S(2)}) copy-start(f32[1,1024]{1,0:T(1,128)S(1)} %convert.11.gain_ref) | copy-start | bytes 12292
  46.5 1.0 copy-start.6
  46.5 38.2 %copy-start.10 = (bf16[512,1024]{1,0:T(8,128)(2,1)}, bf16[512,1024]{1,0:T(8,128)(2,1)S(1)}, u32[]{:S(2)}) copy-start(bf16[512,1024]{1,0:T(8,128)(2,1)S(1)} %get-tuple-element.45.xn_ref) | copy-start | bytes 3145732
  46.5 61.6 %copy-start.9 = (f32[512,128]{1,0:T(8,128)}, f32[512,128]{1,0:T(8,128)S(1)}, u32[]{:S(2)}) copy-start(f32[512,128]{1,0:T(8,128)S(1)} %get-tuple-element.48.dbc_ref) | copy-start | bytes 786436
  46.6 61.6 %copy-start.8 = (f32[16,2048]{1,0:T(8,128)}, f32[16,2048]{1,0:T(8,128)S(1)}, u32[]{:S(2)}) copy-start(f32[16,2048]{1,0:T(8,128)S(1)} %broadcast_multiply_fusion.rate_ref.rate2_ref) | copy-start | bytes 393220
  46.6 61.5 %copy-start.4 = (bf16[4,16,8,512]{3,2,0,1:T(8,128)(2,1)}, bf16[4,16,8,512]{3,2,0,1:T(8,128)(2,1)S(1)}, u32[]{:S(2)}) copy-start(bf16[4,16,8,512]{3,2,0,1:T(8,128)(2,1)S(1)} %copy.45) | copy-start | bytes 1572868
  47.5 1.6 copy-start
  262.1 4.2 %copy-start.14 = (bf16[2,2,2,64,1024]{4,3,2,1,0:T(8,128)(2,1)S(1)}, bf16[2,2,2,64,1024]{4,3,2,1,0:T(8,128)(2,1)}, u32[]{:S(2)}) copy-start(bf16[2,2,2,64,1024]{4,3,2,1,0:T(8,128)(2,1)} %get-tuple-element.73) | copy-start | bytes 3145732
  262.1 5.9 %copy-start.15 = (bf16[2,2,2,32,512]{4,3,2,1,0:T(8,128)(2,1)S(1)}, bf16[2,2,2,32,512]{4,3,2,1,0:T(8,128)(2,1)}, u32[]{:S(2)}) copy-start(bf16[2,2,2,32,512]{4,3,2,1,0:T(8,128)(2,1)} %get-tuple-element.70) | copy-start | bytes 786436
  262.2 9.7 %copy-start.13 = (f32[512,1024]{1,0:T(8,128)S(1)}, f32[512,1024]{1,0:T(8,128)}, u32[]{:S(2)}) copy-start(f32[512,1024]{1,0:T(8,128)} %get-tuple-element.98) | copy-start | bytes 6291460

commit v2 on v1

--- a/solution.py
+++ b/solution.py
@@ -10,38 +10,27 @@
 QLEN = 16
 LANES = 128
 WIDE = 256
-SPREAD_TIMES = (4, 7, 11)
-INNER_TIMES = (0, 1, 4, 6, 7, 8, 9, 10, 12)
-SMALL_TIMES = (0, 1, 3, 4, 5, 6, 7, 8, 9)
+SPREAD_TIMES = ((4.02, 7.06, 13.1), (6.02, 12.02, 13.16))
+INNER_TIMES = (
+    (1, 3.02, 7.04, 12.04, 13.2, 13.32, 13.44, 13.52, 13.62),
+    (3, 4.04, 10.04, 13.02, 13.12, 13.28, 13.42, 13.48, 13.6),
+    (5, 7.02, 13.06, 13.22, 13.34, 13.46, 13.58, 13.7, 13.78),
+    (7, 9.02, 13.08, 13.24, 13.36, 13.5, 13.64, 13.72, 13.8),
+)
+SMALL_TIMES = ((7, 10.02, 13.14, 13.26, 13.38, 13.54, 13.66, 13.74, 13.82),)
+GAIN_TIMES = ((12.01, 13.04, 13.18, 13.3, 13.4, 13.56, 13.68, 13.76, 13.84),)
+DXN_TIMES = (8, 9.5, 10.5, 11.5)
+NORM_TIME = 12
 NEVER = 1e30
 LOG2E = 1.4426950408889634
 FORWARD_STEPS = (0, 4, 7, 9, 12, 14)
-BACKWARD_TIMES = (0, 3, 8, 11, 13, 16)
+BACKWARD_TIMES = (
+    ((0, 2.1, 6.1, 9.1, 11.1, 13.1), (0, 3.1, 7.1, 10.1, 12.1, 14.1)),
+    ((0, 4.1, 8.1, 11.2, 13.2, 15.1), (0, 5.1, 9.2, 12.2, 14.2, 16.1)),
+)
 
 
 EPSILON = 1e-05
-
-
-def shifted_down(values, offset):
-    padding = jnp.zeros((offset,) + values.shape[1:], values.dtype)
-    return jnp.concatenate([padding, values[:-offset]], axis=0)
-
-
-def protein_masks(lens_row, start_row, length, taps):
-    protein_ends = jnp.cumsum(lens_row)
-    protein_begins = protein_ends - lens_row
-    flagged = (start_row > 0) & (lens_row > 0)
-    position = jnp.arange(length, dtype=jnp.int32)
-    cluster = jnp.sum(
-        ((position[:, None] >= protein_begins[None, :]) & flagged[None, :]).astype(jnp.int32),
-        axis=1,
-    )
-    live_mask = (position < protein_ends[-1]).astype(jnp.float32)
-    same_masks = []
-    for offset in range(1, taps):
-        matching = (position >= offset) & (cluster == shifted_down(cluster, offset))
-        same_masks.append(matching.astype(jnp.float32))
-    return (live_mask, same_masks)
 
 
 def rows_product(left, right):
@@ -114,8 +103,8 @@
 
 
 class Gather:
-    def __init__(self, shards, outs, scratch):
-        self.shards, self.outs = shards, outs
+    def __init__(self, shards, outs, scratch, made=None):
+        self.shards, self.outs, self.made = shards, outs, made
         self.count = len(shards)
         self.stage = scratch[: self.count]
         self.load_sem, self.core_sem, self.hop_sem, self.whole_sem = scratch[self.count :]
@@ -148,16 +137,22 @@
     def load(self, a):
         return pltpu.make_async_copy(self.shards[a], self.stage[a], self.load_sem.at[a])
 
+    def in_place(self, a):
+        return self.made is not None and a == self.count - 1
+
     def store(self, a):
         return pltpu.make_async_copy(self.stage[a], self.outs[a].at[self.mine], self.load_sem.at[a])
 
     def begin(self):
         greet(self.own, ("core", "pair", "bit", "low"))
-        for half in range(2):
-            for a in range(self.count):
+        for a in range(self.count):
+            if self.in_place(a):
+                self.made()
+            for half in range(2):
                 self.link.send(functools.partial(self.to_pair, a, half))
         for a in range(self.count):
-            self.load(a).start()
+            if not self.in_place(a):
+                self.load(a).start()
             self.link.send(functools.partial(self.own_to_core, a))
 
     def to_pair(self, a, half):
@@ -188,7 +183,8 @@
             self.pass_on(a, 0, half, 2, "low")
         if half == 1:
             for a in range(self.count):
-                self.load(a).wait()
+                if not self.in_place(a):
+                    self.load(a).wait()
                 self.store(a).start()
 
     def from_near(self, half):
@@ -216,35 +212,64 @@
         self.link.finish()
 
     @staticmethod
-    def scratch(shards):
-        count = len(shards)
+    def scratch(shapes):
+        count = len(shapes)
         dma = pltpu.SemaphoreType.DMA
-        staged = [pltpu.VMEM(s.shape, s.dtype) for s in shards]
+        staged = [pltpu.VMEM(shape, jnp.bfloat16) for shape in shapes]
         return staged + [dma((count,)), dma((2, count, 4, 2)), dma((2, count, 4, 2)), dma((2, count))]
 
 
-def gather_kernel(count, *refs):
-    for stage in Gather(refs[:count], refs[count : 2 * count], refs[2 * count :]).stages:
+def gather_kernel(
+    width, in_ref, dtproj_ref, alog_ref, xproj_ref, taps_ref, bias_ref, step_ref, skip_ref, gain_ref, inner_out, packed_out, *scratch
+):
+    packed = scratch[1]
+
+    def pack():
+        low = packed.dtype
+        rank, states, columns = dtproj_ref.shape[0], alog_ref.shape[0], xproj_ref.shape[1]
+        eye = (
+            lax.broadcasted_iota(jnp.int32, (columns, columns), 0) == lane_index((columns, columns))
+        ).astype(low)
+        at = rank + states + columns
+        owned = packed.shape[1]
+        wide = jnp.float32
+        packed[:rank, :] = dtproj_ref[...]
+        packed[rank : rank + states, :] = alog_ref[...]
+        packed[rank + states : at, :] = transposed_product(eye, xproj_ref[...]).astype(low)
+        row = lax.broadcasted_iota(jnp.int32, (16, owned), 0)
+        rows = jnp.concatenate([taps_ref[...].astype(wide), jnp.zeros((16 - TAPS, owned), wide)], axis=0)
+        for place, ref in ((BIAS_ROW, bias_ref), (STEP_ROW, step_ref), (SKIP_ROW, skip_ref), (GAIN_ROW, gain_ref)):
+            values = ref[...].astype(wide).reshape(1, ref.shape[0])
+            if ref.shape[0] < owned:
+                values = jnp.concatenate([values, jnp.zeros((1, owned - ref.shape[0]), wide)], axis=1)
+            rows = jnp.where(row == place, values, rows)
+        packed[at : at + 16, :] = rows.astype(low)
+        packed[at + 16 :, :] = jnp.zeros((packed.shape[0] - at - 16, owned), low)
+
+    gather = Gather((in_ref.at[:, pl.ds(0, width)], packed), (inner_out, packed_out), scratch, made=pack)
+    for stage in gather.stages:
         stage()
 
 
-def gathered_shape(shard):
-    return jax.ShapeDtypeStruct((4,) + shard.shape, shard.dtype)
-
-
-def gather_weights(shards, collective_id):
-    count = len(shards)
+def gathered_shape(shape):
+    return jax.ShapeDtypeStruct((4,) + shape, jnp.bfloat16)
+
+
+def gather_weights(in_w, dtproj_w, a_log, xproj_w, conv_w, vectors, collective_id):
+    anywhere, vmem = pl.BlockSpec(memory_space=pl.ANY), pl.BlockSpec(memory_space=pltpu.VMEM)
+    used = dtproj_w.shape[0] + a_log.shape[0] + xproj_w.shape[1] + TAPS + len(vectors)
+    shapes = [(in_w.shape[0], in_w.shape[1] // 2), (used + -used % LANES, conv_w.shape[1])]
     return pl.pallas_call(
-        functools.partial(gather_kernel, count),
-        out_shape=[gathered_shape(s) for s in shards],
-        in_specs=[pl.BlockSpec(memory_space=pl.ANY)] * count,
-        out_specs=[pl.BlockSpec(memory_space=pl.ANY)] * count,
-        scratch_shapes=Gather.scratch(shards),
+        functools.partial(gather_kernel, shapes[0][1]),
+        out_shape=[gathered_shape(shape) for shape in shapes],
+        in_specs=[anywhere] + [vmem] * (4 + len(vectors)),
+        out_specs=[anywhere, anywhere],
+        scratch_shapes=Gather.scratch(shapes),
         compiler_params=pltpu.CompilerParams(
-            collective_id=collective_id, has_side_effects=True, vmem_limit_bytes=32 << 20
+            collective_id=collective_id, has_side_effects=True, vmem_limit_bytes=60 << 20
         ),
         name="gather_weights",
-    )(*shards)
+    )(in_w, dtproj_w, a_log, xproj_w, conv_w, *vectors)
 
 
 def run_stages(stages, at_steps):
@@ -258,15 +283,17 @@
 
 
 DIMS = ("pair", "high", "low", "bit")
-PARTS = 4
 MIXED = (
     ("pair", "bit", "low", "high"),
     ("bit", "low", "pair", "high"),
     ("low", "pair", "bit", "high"),
     ("pair", "low", "bit", "high"),
 )
-PAIR_FIRST = (("pair", "bit", "low", "high"), ("pair", "low", "bit", "high")) * 2
-SPREAD = (("high", "low", "bit"), ("high", "bit", "low"), ("high", "low", "bit"), ("high", "low", "bit"))
+PAIR_FIRST = (("pair", "bit", "low", "high"), ("pair", "low", "bit", "high"))
+LOW_FIRST, BIT_FIRST = ("high", "low", "bit"), ("high", "bit", "low")
+EARLY_ORDERS = (MIXED[:2], MIXED[2:])
+TAIL_ORDERS = (None, None, PAIR_FIRST * 2, PAIR_FIRST[:1], PAIR_FIRST[:1])
+TAIL_SPREADS = ((LOW_FIRST,), (BIT_FIRST,), (LOW_FIRST, BIT_FIRST, LOW_FIRST, BIT_FIRST), (LOW_FIRST,), (LOW_FIRST,))
 EVERY = slice(None)
 
 
@@ -282,25 +309,28 @@
     lax.fori_loop(0, 2**free, step, 0)
 
 
-def part_columns(columns, k):
-    return pl.ds(k * (columns // PARTS), columns // PARTS)
-
-
-def region(chosen, dims, columns, k):
-    return tuple(chosen.get(d, EVERY) for d in dims) + (EVERY, part_columns(columns, k))
+def part_columns(columns, parts, k):
+    return pl.ds(k * (columns // parts), columns // parts)
+
+
+def region(chosen, dims, columns):
+    return tuple(chosen.get(d, EVERY) for d in dims) + (EVERY, columns)
 
 
 class Halving:
     def __init__(self, link, orders, local, scratch, given=None):
         self.link, self.own, self.orders, self.local, self.given = link, link.own, orders, local, given
         self.cores, *self.arrived, self.load_sem, self.core_sem, self.half_sem = scratch
-        self.columns = local.shape[-1]
+        self.parts = len(orders)
+
+    def columns(self, k):
+        return part_columns(self.local.shape[-1], self.parts, k)
 
     def lead(self, core):
         return () if self.given is not None else (core,)
 
     def of_pair(self, y, k):
-        return region({"pair": y}, DIMS, self.columns, k)
+        return region({"pair": y}, DIMS, self.columns(k))
 
     def loading(self, k, y):
         at = self.of_pair(y, k)
@@ -330,7 +360,7 @@
             self.link.receive(self.cores.at[self.of_pair(y, k)], sems, "core")
 
         def add(index):
-            at = index + (EVERY, part_columns(self.columns, k))
+            at = index + (EVERY, self.columns(k))
             kept = self.lead(self.own["core"]) + at
             self.local[kept] = self.local[kept] + self.cores[at]
 
@@ -341,7 +371,7 @@
         dim = self.orders[k][step]
         chosen = {d: self.own[d] for d in self.orders[k][:step]}
         chosen[dim] = 1 - self.own[dim]
-        at = self.lead(self.own["core"]) + region(chosen, DIMS, self.columns, k)
+        at = self.lead(self.own["core"]) + region(chosen, DIMS, self.columns(k))
         sems = (self.half_sem.at[0, k, step], self.half_sem.at[1, k, step])
         return self.local.at[at], self.arrived[step].at[k], sems, dim
 
@@ -356,7 +386,7 @@
 
         def add(index):
             at = tuple(chosen[d] if d in chosen else index[free.index(d)] for d in DIMS)
-            kept = self.lead(self.own["core"]) + at + (EVERY, part_columns(self.columns, k))
+            kept = self.lead(self.own["core"]) + at + (EVERY, self.columns(k))
             total = self.local[kept] + self.arrived[step][(k,) + index + (EVERY, EVERY)]
             if step < 3:
                 self.local[kept] = total
@@ -368,44 +398,48 @@
             self.halve(k, step + 1)
 
     @staticmethod
-    def scratch(rows, columns):
+    def scratch(shape, parts):
+        rows, columns = shape
         dma = pltpu.SemaphoreType.DMA
         low = jnp.bfloat16
         shapes = [pltpu.VMEM((2, 2, 2, 2, rows, columns), low)]
-        shapes += [pltpu.VMEM((PARTS,) + (2,) * (3 - step) + (rows, columns // PARTS), low) for step in range(4)]
-        return shapes + [dma((PARTS, 2)), dma((2, PARTS, 2)), dma((2, PARTS, 4))]
+        shapes += [pltpu.VMEM((parts,) + (2,) * (3 - step) + (rows, columns // parts), low) for step in range(4)]
+        return shapes + [dma((parts, 2)), dma((2, parts, 2)), dma((2, parts, 4))]
 
 
 class Spreading:
-    def __init__(self, link, full, sems):
-        self.link, self.own, self.full, self.sems = link, link.own, full, sems
-        self.columns = full.shape[-1]
+    def __init__(self, link, orders, full, sems):
+        self.link, self.own, self.orders, self.full, self.sems = link, link.own, orders, full, sems
+        self.parts = len(orders)
+
+    def columns(self, k):
+        return part_columns(self.full.shape[-1], self.parts, k)
 
     def put(self, k, value):
-        at = tuple(self.own[d] for d in DIMS[1:]) + (EVERY, part_columns(self.columns, k))
+        at = tuple(self.own[d] for d in DIMS[1:]) + (EVERY, self.columns(k))
         self.full[at] = value
         self.pass_on(k, 0)
 
     def held(self, k, step):
-        chosen = {d: self.own[d] for d in SPREAD[k][step:]}
-        here = self.full.at[region(chosen, DIMS[1:], self.columns, k)]
-        return here, here, (self.sems.at[0, k, step], self.sems.at[1, k, step]), SPREAD[k][step]
+        chosen = {d: self.own[d] for d in self.orders[k][step:]}
+        here = self.full.at[region(chosen, DIMS[1:], self.columns(k))]
+        return here, here, (self.sems.at[0, k, step], self.sems.at[1, k, step]), self.orders[k][step]
 
     def pass_on(self, k, step):
         self.link.send(functools.partial(self.held, k, step))
 
     def take(self, k, step):
-        dim = SPREAD[k][step]
-        chosen = {d: self.own[d] for d in SPREAD[k][step:]}
+        dim = self.orders[k][step]
+        chosen = {d: self.own[d] for d in self.orders[k][step:]}
         chosen[dim] = 1 - self.own[dim]
-        there = self.full.at[region(chosen, DIMS[1:], self.columns, k)]
+        there = self.full.at[region(chosen, DIMS[1:], self.columns(k))]
         self.link.receive(there, (self.sems.at[0, k, step], self.sems.at[1, k, step]), dim)
         if step < 2:
             self.pass_on(k, step + 1)
 
     @staticmethod
-    def scratch(rows, columns):
-        return [pltpu.VMEM((2, 2, 2, rows, columns), jnp.bfloat16), pltpu.SemaphoreType.DMA((2, PARTS, 3))]
+    def scratch(shape, parts):
+        return [pltpu.VMEM((2, 2, 2) + shape, jnp.bfloat16), pltpu.SemaphoreType.DMA((2, parts, 3))]
 
 
 def run_events(events, last):
@@ -441,9 +475,30 @@
 BIAS_ROW, STEP_ROW, SKIP_ROW, GAIN_ROW = 4, 5, 6, 7
 
 
-def front_kernel(tokens_ref, gain_ref, w_ref, rows_ref, xproj_ref, mask_ref, inner_ref, pre_ref, u_ref, dbc_ref, xn_ref, xnt_ref):
+def row_masks(lens_ref, start_ref, length):
+    shape = (length, LANES)
+    position = lax.broadcasted_iota(jnp.int32, shape, 0)
+    cluster = jnp.zeros(shape, jnp.int32)
+    begin = 0
+    for slot in range(lens_ref.shape[1]):
+        size = lens_ref[0, slot]
+        flag = jnp.where((start_ref[0, slot] > 0) & (size > 0), 1, 0)
+        cluster = cluster + jnp.where(position >= begin, flag, 0)
+        begin = begin + size
+    lane = lane_index(shape)
+    masks = jnp.where((lane == 0) & (position < begin), 1.0, 0.0)
+    for offset in range(1, TAPS):
+        same = (lane == offset) & (position >= offset) & (cluster == pltpu.roll(cluster, offset, 0))
+        masks = jnp.where(same, 1.0, masks)
+    return masks
+
+
+def front_kernel(
+    lens_ref, start_ref, tokens_ref, gain_ref, w_ref, rows_ref, xproj_ref, inner_ref, pre_ref, u_ref, dbc_ref, xn_ref, xnt_ref, mask_ref
+):
     @pl.when(pl.program_id(0) == 0)
     def _():
+        mask_ref[...] = row_masks(lens_ref, start_ref, mask_ref.shape[0])
         x = tokens_ref[...].astype(jnp.float32)
         inv = lax.rsqrt(jnp.mean(x * x, axis=1, keepdims=True) + EPSILON)
         xn = (x * inv * gain_ref[...]).astype(jnp.bfloat16)
@@ -476,7 +531,7 @@
     return pl.BlockSpec((block, columns), lambda i: (i, 0))
 
 
-def front(tokens, gain, inner_w, by_channel, xproj_t, masks, block=512):
+def front(lens, starts, tokens, gain, inner_w, by_channel, xproj_t, block=512):
     length, features = tokens.shape
     width = inner_w.shape[1]
     low, wide = jnp.bfloat16, jnp.float32
@@ -484,12 +539,13 @@
         front_kernel,
         grid=(width // block,),
         in_specs=[
+            pl.BlockSpec(memory_space=pltpu.SMEM),
+            pl.BlockSpec(memory_space=pltpu.SMEM),
             whole_spec(tokens.shape),
             whole_spec(gain.shape),
             columns_spec(features, block),
             columns_spec(by_channel.shape[0], block),
             columns_spec(LANES, block),
-            whole_spec(masks.shape),
         ],
         out_specs=[
             columns_spec(length, block),
@@ -498,6 +554,7 @@
             whole_spec((length, LANES)),
             whole_spec((length, features)),
             whole_spec((features, length)),
+            whole_spec((length, LANES)),
         ],
         out_shape=[
             jax.ShapeDtypeStruct((length, width), low),
@@ -506,10 +563,11 @@
             jax.ShapeDtypeStruct((length, LANES), wide),
             jax.ShapeDtypeStruct((length, features), low),
             jax.ShapeDtypeStruct((features, length), low),
-        ],
-        compiler_params=pltpu.CompilerParams(vmem_limit_bytes=48 << 20),
+            jax.ShapeDtypeStruct((length, LANES), wide),
+        ],
+        compiler_params=pltpu.CompilerParams(vmem_limit_bytes=60 << 20),
         name="front",
-    )(tokens, gain, inner_w, by_channel, xproj_t, masks)
+    )(lens, starts, tokens, gain, inner_w, by_channel, xproj_t)
 
 
 def spread_states(dbc, first, states):
@@ -544,7 +602,8 @@
     blocks, _, width = long_s.shape
     states = rate_ref.shape[0]
     span = QLEN * states
-    gather = Gather(shards, outs, scratch)
+    in_ref, out_ref = shards
+    gather = Gather((in_ref.at[:, pl.ds(width, width)], out_ref), outs, scratch)
     run_stages(gather.stages[:-1], FORWARD_STEPS)
 
     @pl.when(pl.program_id(0) == 0)
@@ -592,6 +651,7 @@
 
 def scan_forward(rank, u, dbc, masks, by_channel, dtproj, rate2, shards, collective_id, blocks=2, group=2):
     count = len(shards)
+    shapes = [(shards[0].shape[0], shards[0].shape[1] // 2), shards[1].shape]
     anywhere = [pl.BlockSpec(memory_space=pl.ANY)] * count
     tokens, width = u.shape
     states = rate2.shape[0]
@@ -613,7 +673,7 @@
             jax.ShapeDtypeStruct((tokens, width), jnp.float32),
             jax.ShapeDtypeStruct((tokens * states, width), jnp.bfloat16),
             jax.ShapeDtypeStruct((tokens, width), jnp.float32),
-            *(gathered_shape(s) for s in shards),
+            *(gathered_shape(shape) for shape in shapes),
         ],
         scratch_shapes=[
             pltpu.VMEM((states, width), jnp.float32),
@@ -621,10 +681,10 @@
             pltpu.VMEM((blocks, QLEN, width), jnp.float32),
             pltpu.VMEM((rows * states, LANES), jnp.float32),
             pltpu.VMEM((rows, QLEN * states), jnp.bfloat16),
-            *Gather.scratch(shards),
+            *Gather.scratch(shapes),
         ],
         compiler_params=pltpu.CompilerParams(
-            collective_id=collective_id, has_side_effects=True, vmem_limit_bytes=48 << 20
+            collective_id=collective_id, has_side_effects=True, vmem_limit_bytes=60 << 20
         ),
         name="scan_forward",
     )(u, dbc, masks, by_channel, dtproj, rate2, *shards)
@@ -704,7 +764,7 @@
             jax.ShapeDtypeStruct(tokens.shape, wide),
         ],
         scratch_shapes=[pltpu.VMEM(tokens.shape, wide), pltpu.VMEM(tokens.shape, low)],
-        compiler_params=pltpu.CompilerParams(vmem_limit_bytes=56 << 20),
+        compiler_params=pltpu.CompilerParams(vmem_limit_bytes=60 << 20),
         name="middle",
     )(xn, xnt, gate_w, y, u, by_channel, out_w, cotangent, tokens, masks)
 
@@ -722,20 +782,17 @@
     halvings = []
     for a in range(count):
         local, *scratch = refs[13 + a * per : 13 + (a + 1) * per]
-        halvings.append(Halving(link, MIXED, local, scratch, given=grads[a]))
-
-    def keep_sum(out, k, total):
-        out[:, part_columns(out.shape[1], k)] = total
+        halvings.append(Halving(link, EARLY_ORDERS[a], local, scratch, given=grads[a]))
+
+    def keep_sum(out, parts, k, total):
+        out[:, part_columns(out.shape[1], parts, k)] = total
 
     events = [(0, lambda: greet(link.own, ("core", "pair", "bit", "low", "high")))]
-    for k in range(PARTS):
-        for halving, out in zip(halvings, sums):
-            give, join, *times = BACKWARD_TIMES
+    for halving, out, part_times in zip(halvings, sums, BACKWARD_TIMES):
+        done = functools.partial(keep_sum, out, halving.parts)
+        for k, (give, join, *times) in enumerate(part_times):
             events += [(give, functools.partial(halving.give, k)), (join, functools.partial(halving.join, k))]
-            events += [
-                (time, functools.partial(halving.halved, k, step, functools.partial(keep_sum, out)))
-                for step, time in enumerate(times)
-            ]
+            events += [(time, functools.partial(halving.halved, k, step, done)) for step, time in enumerate(times)]
     final = steps - 1
     run_events([event for event in events if event[0] <= final], final)
 
@@ -896,12 +953,12 @@
             pltpu.VMEM((rows, LANES), wide),
             *(
                 shape
-                for g in grads
-                for shape in (pltpu.VMEM((2, 2, 2, 2) + g.shape[4:], low), *Halving.scratch(*g.shape[4:]))
+                for g, orders in zip(grads, EARLY_ORDERS)
+                for shape in (pltpu.VMEM((2, 2, 2, 2) + g.shape[4:], low), *Halving.scratch(g.shape[4:], len(orders)))
             ),
         ],
         compiler_params=pltpu.CompilerParams(
-            collective_id=collective_id, has_side_effects=True, vmem_limit_bytes=56 << 20
+            collective_id=collective_id, has_side_effects=True, vmem_limit_bytes=60 << 20
         ),
         name="scan_backward",
     )(u, in_blocks(dt), in_blocks(d_y), dbc, masks, h, h, by_channel, dtproj, rate2, rate, *grads)
@@ -913,47 +970,74 @@
     dtproj_ref, alog_ref, bias_ref, skip_ref, *refs
 ):
     wide, low = jnp.float32, jnp.bfloat16
-    pieces, tokengrad_ref, outs = refs[:count], refs[count], refs[count + 1 : 2 * count + 3]
-    refs = refs[2 * count + 3 :]
-    dxn, xproj_s, row_s, inner_s, small_s, out_sem = refs[:6]
+    pieces, tokengrad_ref, outs = refs[:count], refs[count], refs[count + 1 : 2 * count + 4]
+    refs = refs[2 * count + 4 :]
+    w_s, x_s, cot_s, dxn, dinner_s, xproj_s, row_s, inner_s, small_s, gain_s, load_sem, out_sem = refs[:12]
     link = Link(own_bits())
-    halving_refs, spreading_refs = refs[6 : 6 + 16], refs[6 + 16 :]
-    spreadings = [Spreading(link, *spreading_refs[2 * a : 2 * a + 2]) for a in range(count + 2)]
-    inner_sum = Halving(link, PAIR_FIRST, inner_s, halving_refs[:8])
-    small_sum = Halving(link, PAIR_FIRST, small_s, halving_refs[8:])
+    halving_refs, spreading_refs = refs[12 : 12 + 24], refs[12 + 24 :]
+    spreadings = [Spreading(link, orders, *spreading_refs[2 * a : 2 * a + 2]) for a, orders in enumerate(TAIL_SPREADS)]
+    inner_sum = Halving(link, TAIL_ORDERS[2], inner_s, halving_refs[:8])
+    small_sum = Halving(link, TAIL_ORDERS[3], small_s, halving_refs[8:16])
+    gain_sum = Halving(link, TAIL_ORDERS[4], gain_s, halving_refs[16:])
     block = du_ref.shape[1]
     here = pl.program_id(0)
     columns = pl.ds(pl.multiple_of(here * block, block), block)
     final = steps - 1
 
+    loads = [(w_ref, w_s), (tokens_ref, x_s), (cot_ref, cot_s), (dgate_ref, dxn)]
+    loads = [functools.partial(pltpu.make_async_copy, src, dst, load_sem.at[i]) for i, (src, dst) in enumerate(loads)]
+
     def start():
+        for load in loads:
+            load().start()
         greet(link.own, ("core", "pair", "bit", "low", "high"))
-        for k in range(PARTS):
-            for piece, spreading in zip(pieces, spreadings):
-                spreading.put(k, piece[:, part_columns(piece.shape[1], k)])
-
-    def add_up(events, halving, spreading, k, first, times):
-        give, join, *halves = times[:6]
-        events += [(first + give, functools.partial(halving.give, k)), (first + join, functools.partial(halving.join, k))]
-        events += [
-            (first + time, functools.partial(halving.halved, k, step, spreading.put)) for step, time in enumerate(halves)
-        ]
-        events += [
-            (first + time, functools.partial(spreading.take, k, step)) for step, time in enumerate(times[6:])
-        ]
+        for piece, spreading in zip(pieces, spreadings):
+            for k in range(spreading.parts):
+                spreading.put(k, piece[:, spreading.columns(k)])
+
+    def add_up(events, halving, spreading, part_times):
+        for k, times in enumerate(part_times):
+            give, join, *halves = times[:6]
+            events += [(give, functools.partial(halving.give, k)), (join, functools.partial(halving.join, k))]
+            events += [
+                (time, functools.partial(halving.halved, k, step, spreading.put)) for step, time in enumerate(halves)
+            ]
+            events += [(time, functools.partial(spreading.take, k, step)) for step, time in enumerate(times[6:])]
 
     events = []
-    for k in range(PARTS):
-        for spreading in spreadings[:count]:
-            events += [(time, functools.partial(spreading.take, k, step)) for step, time in enumerate(SPREAD_TIMES)]
-        ready = (k + 1) * steps // PARTS - 1
-        add_up(events, inner_sum, spreadings[count], k, ready, INNER_TIMES)
-        add_up(events, small_sum, spreadings[count + 1], k, final, SMALL_TIMES)
+    for spreading, times in zip(spreadings, SPREAD_TIMES):
+        events += [(time, functools.partial(spreading.take, 0, step)) for step, time in enumerate(times)]
+    add_up(events, inner_sum, spreadings[count], INNER_TIMES)
+    add_up(events, small_sum, spreadings[count + 1], SMALL_TIMES)
+    add_up(events, gain_sum, spreadings[count + 2], GAIN_TIMES)
+
+    def through_inner(chunk):
+        if chunk == 0:
+            for load in loads:
+                load().wait()
+        size = dinner_s.shape[1] // len(DXN_TIMES)
+        own = slice(chunk * size, (chunk + 1) * size)
+        dxn[...] += transposed_product(dinner_s[:, own], w_s[:, own])
+
+    def through_norm():
+        x = x_s[...].astype(wide)
+        inv = lax.rsqrt(jnp.mean(x * x, axis=1, keepdims=True) + EPSILON)
+        x_hat = x * inv
+        gain_grad = jnp.sum(dxn[...] * x_hat, axis=0, keepdims=True)
+        d_hat = dxn[...] * gain_ref[...]
+        level = jnp.mean(d_hat * x_hat, axis=1, keepdims=True)
+        tokengrad_ref[...] = cot_s[...].astype(wide) + inv * (d_hat - x_hat * level)
+        size = gain_grad.shape[1] // 4
+        rows, lanes = gain_s.shape[5:]
+        gain_s[...] = jnp.zeros_like(gain_s)
+        for shard in range(4):
+            parts = [gain_grad[:, c : c + lanes] for c in range(shard * size, (shard + 1) * size, lanes)]
+            block = jnp.concatenate(parts + [jnp.zeros((rows - len(parts), lanes), wide)], axis=0)
+            gain_s[shard % 2, shard // 2, 0, 0, 0] = block.astype(low)
+
+    events += [(time, functools.partial(through_inner, chunk)) for chunk, time in enumerate(DXN_TIMES)]
+    events.append((NORM_TIME, through_norm))
     run_events([(0, start)], final)
-
-    @pl.when(here == 0)
-    def _():
-        dxn[...] = dgate_ref[...]
 
     rows = rows_ref[...]
     pre = pre_ref[...]
@@ -979,28 +1063,17 @@
     for shard in range(4):
         own_rows = inner_grad[shard * size : (shard + 1) * size]
         inner_s[shard % 2, shard // 2, :, :, :, :, columns] = own_rows.reshape(2, 2, 2, size // 8, block)
-    dxn[...] += transposed_product(d_inner, w_ref[...])
+    dinner_s[:, columns] = d_inner
 
     @pl.when(here == final)
     def _():
-        x = tokens_ref[...].astype(wide)
-        inv = lax.rsqrt(jnp.mean(x * x, axis=1, keepdims=True) + EPSILON)
-        x_hat = x * inv
-        gain_grad = jnp.sum(dxn[...] * x_hat, axis=0, keepdims=True)
-        d_hat = dxn[...] * gain_ref[...]
-        level = jnp.mean(d_hat * x_hat, axis=1, keepdims=True)
-        tokengrad_ref[...] = cot_ref[...].astype(wide) + inv * (d_hat - x_hat * level)
         owned = xproj_s.shape[1] // 4
         states = alog_ref.shape[0]
-        part = gain_grad.shape[1] // 4
         row = lax.broadcasted_iota(jnp.int32, (8, owned), 0)
         for shard in range(4):
             own = slice(shard * owned, (shard + 1) * owned)
-            gains = jnp.concatenate(
-                [gain_grad[:, shard * part : (shard + 1) * part], jnp.zeros((1, owned - part), wide)], axis=1
-            )
             rows = row_s[:, own]
-            for at, extra in ((STEP_ROW, bias_ref[:, own]), (SKIP_ROW, skip_ref[:, own]), (GAIN_ROW, gains)):
+            for at, extra in ((STEP_ROW, bias_ref[:, own]), (SKIP_ROW, skip_ref[:, own])):
                 rows = jnp.where(row == at, extra, rows)
             stacked = [dtproj_ref[:rank, own], alog_ref[:, own], xproj_s[: rank + 2 * states, own], rows]
             height = 8 * small_s.shape[5]
@@ -1031,7 +1104,8 @@
     inner_shape = (features // 32, width)
     used = 2 * rank + 3 * alog_grad.shape[0] + 8
     small_shape = ((used + -used % LANES) // 8, width // 4)
-    shapes = [*(p.shape for p in pieces), inner_shape, small_shape]
+    gain_shape = (16, LANES)
+    shapes = [*(p.shape for p in pieces), inner_shape, small_shape, gain_shape]
     low, wide = jnp.bfloat16, jnp.float32
     channels = columns_spec(length, block)
     token_grad, *sums = pl.pallas_call(
@@ -1047,10 +1121,7 @@
             columns_spec(by_channel.shape[0], block),
             whole_spec(masks.shape),
             whole_spec(xnt.shape),
-            columns_spec(features, block),
-            whole_spec(dxn_gate.shape),
-            whole_spec(tokens.shape),
-            whole_spec(tokens.shape),
+            *[pl.BlockSpec(memory_space=pl.ANY)] * 4,
             whole_spec(gain.shape),
             whole_spec(dtproj_grad.shape),
             whole_spec(alog_grad.shape),
@@ -1058,24 +1129,31 @@
             whole_spec(skip_grad.shape),
             *(whole_spec(p.shape) for p in pieces),
         ],
-        out_specs=[whole_spec(tokens.shape), *[pl.BlockSpec(memory_space=pl.ANY)] * (count + 2)],
+        out_specs=[whole_spec(tokens.shape), *[pl.BlockSpec(memory_space=pl.ANY)] * (count + 3)],
         out_shape=[
             jax.ShapeDtypeStruct(tokens.shape, wide),
             *(jax.ShapeDtypeStruct((2, 2, 2) + shape, low) for shape in shapes),
         ],
         scratch_shapes=[
+            pltpu.VMEM(inner_w.shape, low),
+            pltpu.VMEM(tokens.shape, low),
+            pltpu.VMEM(tokens.shape, low),
             pltpu.VMEM(tokens.shape, wide),
+            pltpu.VMEM((length, width), low),
             pltpu.VMEM((LANES, width), wide),
             pltpu.VMEM((8, width), wide),
             pltpu.VMEM((2, 2, 2, 2, 2) + inner_shape, low),
             pltpu.VMEM((2, 2, 2, 2, 2) + small_shape, low),
-            pltpu.SemaphoreType.DMA((count + 2,)),
-            *Halving.scratch(*inner_shape),
-            *Halving.scratch(*small_shape),
-            *(shape for s in shapes for shape in Spreading.scratch(*s)),
+            pltpu.VMEM((2, 2, 2, 2, 2) + gain_shape, low),
+            pltpu.SemaphoreType.DMA((4,)),
+            pltpu.SemaphoreType.DMA((count + 3,)),
+            *Halving.scratch(inner_shape, len(TAIL_ORDERS[2])),
+            *Halving.scratch(small_shape, len(TAIL_ORDERS[3])),
+            *Halving.scratch(gain_shape, len(TAIL_ORDERS[4])),
+            *(v for shape, orders in zip(shapes, TAIL_SPREADS) for v in Spreading.scratch(shape, len(orders))),
         ],
         compiler_params=pltpu.CompilerParams(
-            collective_id=collective_id, has_side_effects=True, vmem_limit_bytes=58 << 20
+            collective_id=collective_id, has_side_effects=True, vmem_limit_bytes=60 << 20
         ),
         name="tail",
     )(
@@ -1083,6 +1161,59 @@
         dtproj_grad, alog_grad, bias_grad, skip_grad, *pieces,
     )
     return token_grad, sums
+
+
+def finish_kernel(
+    rank, states, gate_ref, out_ref, inner_ref, small_ref, gain_ref,
+    in_grad, out_grad, dtproj_grad, alog_grad, xproj_grad, conv_grad, convb_grad, dtb_grad, skip_grad, gain_grad
+):
+    wide = jnp.float32
+    width = inner_ref.shape[1]
+    in_grad[:, :width] = inner_ref[...].astype(wide)
+    in_grad[:, width:] = gate_ref[...].astype(wide)
+    out_grad[...] = out_ref[...].astype(wide)
+
+    @pl.when(pl.program_id(0) == 0)
+    def _():
+        small = small_ref[...].astype(wide)
+        used = 2 * rank + 3 * states
+        dtproj_grad[...] = small[:rank]
+        alog_grad[...] = small[rank : rank + states]
+        xproj_grad[...] = small[rank + states : rank + states + LANES].T[:, : rank + 2 * states]
+        rows = small[used : used + 8]
+        conv_grad[...] = rows[:TAPS]
+        for ref, row in ((convb_grad, BIAS_ROW), (dtb_grad, STEP_ROW), (skip_grad, SKIP_ROW)):
+            ref[...] = rows[row : row + 1]
+        for part in range(gain_grad.shape[1] // LANES):
+            gain_grad[:, part * LANES : (part + 1) * LANES] = gain_ref[part : part + 1, :].astype(wide)
+
+
+def finish(rank, states, gate, out, inner, small, gain, features, steps=4):
+    wide = jnp.float32
+    owned = small.shape[1]
+    width = inner.shape[1]
+    small_shapes = [(rank, owned), (states, owned), (owned, rank + 2 * states), (TAPS, owned)]
+    small_shapes += [(1, owned)] * 3 + [(1, features)]
+    in_shape, out_shape = (inner.shape[0], 2 * width), out.shape
+    return pl.pallas_call(
+        functools.partial(finish_kernel, rank, states),
+        grid=(steps,),
+        in_specs=[
+            rows_spec(gate.shape[0] // steps, width),
+            rows_spec(out.shape[0] // steps, out.shape[1]),
+            rows_spec(inner.shape[0] // steps, width),
+            whole_spec(small.shape),
+            whole_spec(gain.shape),
+        ],
+        out_specs=[
+            rows_spec(in_shape[0] // steps, in_shape[1]),
+            rows_spec(out_shape[0] // steps, out_shape[1]),
+            *(whole_spec(shape) for shape in small_shapes),
+        ],
+        out_shape=[jax.ShapeDtypeStruct(shape, wide) for shape in (in_shape, out_shape, *small_shapes)],
+        compiler_params=pltpu.CompilerParams(vmem_limit_bytes=60 << 20),
+        name="finish",
+    )(gate, out, inner, small, gain)
 
 
 def add_groups(sums):
@@ -1109,20 +1240,12 @@
     d_skip,
     out_w,
 ):
-    length = tokens.shape[0]
     features = norm_gain.shape[0]
     width = in_w.shape[1] // 2
     rank, owned = dtproj_w.shape
     states = a_log.shape[0]
-    live_mask, same_masks = protein_masks(prot_lens[0], clus_start[0], length, TAPS)
-    masks = jnp.stack([live_mask, *same_masks], axis=1)
-    fill = lambda v: jnp.pad(v, ((0, 0), (0, owned - v.shape[1])))
-    packed = jnp.concatenate(
-        [dtproj_w, a_log, xproj_w.T, conv_w, conv_b[None], dt_bias[None], d_skip[None], fill(norm_gain[None])], axis=0
-    )
-    used = packed.shape[0]
-    packed = jnp.pad(packed, ((0, -used % LANES), (0, 0)))
-    inner_w, packed = gather_weights((in_w[:, :width], packed), 1)
+    used = 2 * rank + 3 * states + 8
+    inner_w, packed = gather_weights(in_w, dtproj_w, a_log, xproj_w, conv_w, (conv_b, dt_bias, d_skip, norm_gain), 1)
     inner_w = inner_w.reshape(-1, width)
     gain = packed[:, used - 1, :features].reshape(1, -1).astype(jnp.float32)
     packed = jnp.swapaxes(packed, 0, 1).reshape(packed.shape[1], -1)
@@ -1131,9 +1254,9 @@
     rate2 = decay_rate * LOG2E
     xproj_t = packed[rank + states : rank + states + LANES]
     by_channel = packed[used - 8 : used].astype(jnp.float32)
-    inner, pre, u, dbc, xn, xnt = front(tokens, gain, inner_w, by_channel, xproj_t, masks)
+    inner, pre, u, dbc, xn, xnt, masks = front(prot_lens, clus_start, tokens, gain, inner_w, by_channel, xproj_t)
     y, h, dt, (gate_w, out_full) = scan_forward(
-        rank, u, dbc, masks, by_channel, dtproj, rate2, (in_w[:, width:], out_w), 2
+        rank, u, dbc, masks, by_channel, dtproj, rate2, (in_w, out_w), 2
     )
     gate_w = gate_w.reshape(-1, width)
     out_full = out_full.reshape(-1, out_full.shape[2])
@@ -1179,23 +1302,21 @@
         early_pieces,
         4,
     )
-    in_rows = lambda v: v.reshape(-1, v.shape[-1]).astype(jnp.float32)
-    gate_grad, out_grad, inner_grad, small = add_groups([in_rows(v) for v in sums])
-    in_grad = jnp.concatenate([inner_grad, gate_grad], axis=1)
-    dtproj_grad, alog_grad, xproj_grad = small[:rank], small[rank : rank + states], small[rank + states : used - 8].T
-    conv_grad, convb_grad, dtb_grad, skip_grad = small[used - 8 : used - 4], small[used - 4], small[used - 3], small[used - 2]
+    sums = [v.reshape(-1, v.shape[-1]) for v in sums]
+    grads = add_groups(finish(rank, states, *sums, features))
+    in_grad, out_grad, dtproj_grad, alog_grad, xproj_grad, conv_grad, convb_grad, dtb_grad, skip_grad, gain_grad = grads
     return (
         mixed,
         token_grad,
-        small[used - 1, :features],
+        gain_grad[0],
         in_grad,
         conv_grad,
-        convb_grad,
+        convb_grad[0],
         xproj_grad,
         dtproj_grad,
-        dtb_grad,
+        dtb_grad[0],
         alog_grad,
-        skip_grad,
+        skip_grad[0],
         out_grad,
     )
 

time: 274 us -> 259 us (0.945)
  local copies, waits for them, and re-layouts: 16.7 us -> 9.24 us
  other arithmetic: 11.3 us -> 4.98 us
    pallas_call x2 -> x3, Pallas kernels: 33.3 us -> 43.5 us  [the longest x1 26.3 us: gather_weights(): pl.pallas_call(functools.partial(gather_kernel, shapes[0][1]), out_shape=...]
    pallas_call x1, Pallas kernels: 69.5 us -> 61.7 us  [scan_backward(): pl.pallas_call(functools.partial(backward_kernel, rank, count, steps), gr...]
    pallas_call x1, Pallas kernels: 82.3 us -> 75.7 us  [tail(): pl.pallas_call(functools.partial(tail_kernel, steps, rank, count), grid=(...]
    slice x7 -> x0, local copies, waits for them, and re-layouts: 5.41 us -> none  [the longest x1 1.79 us: body(): in_w[:, width:]]
    concatenate x1 -> x0, other arithmetic: 4.2 us -> none  [body(): in_grad = jnp.concatenate([inner_grad, gate_grad], axis=1)]
    pallas_call x1, Pallas kernels: 35.5 us -> 39.1 us  [scan_forward(): pl.pallas_call(functools.partial(forward_kernel, rank, group, count), gri...]
    concatenate x1 -> x0, local copies, waits for them, and re-layouts: 3.36 us -> none  [body(): jnp.concatenate([dtproj_w, a_log, xproj_w.T, conv_w, conv_b[None], dt_bia...]
    unnamed x48 -> x6, local copies, waits for them, and re-layouts: 5.95 us -> 6.02 us
where the time goes in v2:
time: 259 us; the launch traced here: 258 us
  Pallas kernels  243 us (94%)
  local copies, waits for them, and re-layouts  9.24 us (4%)
  other arithmetic  4.98 us (2%)
    pallas_call x1, Pallas kernels, tail(): pl.pallas_call(functools.partial(tail_kernel, steps, rank, count), grid=(...  75.7 us
    pallas_call x1, Pallas kernels, scan_backward(): pl.pallas_call(functools.partial(backward_kernel, rank, count, steps), gr...  61.7 us
    pallas_call x1, Pallas kernels, scan_forward(): pl.pallas_call(functools.partial(forward_kernel, rank, group, count), gri...  39.1 us
    pallas_call x1, Pallas kernels, gather_weights(): pl.pallas_call(functools.partial(gather_kernel, shapes[0][1]), out_shape=...  26.3 us
    pallas_call x1, Pallas kernels, middle(): pl.pallas_call(middle_kernel, grid=(width // block,), in_specs=[whole_spe...  23.4 us
    pallas_call x1, Pallas kernels, front(): pl.pallas_call(front_kernel, grid=(width // block,), in_specs=[pl.BlockSp...  11.6 us
    unnamed x6, local copies, waits for them, and re-layouts  6.02 us
    pallas_call x1, Pallas kernels, finish(): pl.pallas_call(functools.partial(finish_kernel, rank, states), grid=(step...  5.55 us

profile of v2, /device:TPU:0, one launch (start us, length us, event | category | flops | bytes accessed | tf_op | source)
XLA Modules:
  0.0 258.4 jit_solution(11271724214819417062)
XLA Ops:
  0.6 1.7 copy.26.xproj_ref
  2.3 26.3 %gather_weights.1 = (bf16[4,256,2048]{2,1,0:T(8,128)(2,1)}, bf16[4,256,512]{2,1,0:T(8,128)(2,1)}) custom-call(bf16[256,4096]{1,0:T(8,128)(2,1)} %refs_0_.1, bf16[64,512]{1,0:T(8,128)(2,1)} %dtproj_ref.1, bf16[16,512]{1,0:T(8,128)(2,1)} %alog_ref.1, bf16[512,96]{1,0:T(8,128)(2,1)} %copy.26.xproj_ref, bf16[4,512]{1,0:T(4,128)(2,1)} %taps_ref.1, ...), custom_call_target="tpu_custom_call" | custom-call | tf_op jit(solution)/shard_map/gather_weights/pallas_call | solution.py:262
  28.6 0.8 slice.30
  29.3 0.6 convert.2.rows_ref
  30.0 1.3 slice_bitcast_fusion
  31.3 0.9 copy.31
  32.1 0.7 slice.23
  32.9 0.6 convert.3.gain_ref
  33.5 11.6 %front.1 = (bf16[512,2048]{1,0:T(8,128)(2,1)}, f32[512,2048]{1,0:T(8,128)}, bf16[512,2048]{1,0:T(8,128)(2,1)}, f32[512,128]{1,0:T(8,128)}, bf16[512,1024]{1,0:T(...) custom-call(s32[1,8]{1,0:T(1,128)} %lens_ref.1, s32[1,8]{1,0:T(1,128)} %start_ref.1, ...), custom_call_target="tpu_custom_call" | custom-call | tf_op jit(solution)/shard_map/front/pallas_call | solution.py:538
  45.1 0.9 negate_bitcast_fusion
  46.0 0.7 broadcast_multiply_fusion.rate_ref.rate2_ref
  46.7 0.9 copy.32
  47.5 39.1 %scan_forward.1 = (f32[512,2048]{1,0:T(8,128)}, bf16[8192,2048]{1,0:T(8,128)(2,1)}, f32[512,2048]{1,0:T(8,128)}, bf16[4,256,2048]{2,1,0:T(8,128)(2,1)}, bf16[4,512,1024]{2,1,0:T(8,128)(2,1)}) custom-call(bf16[512,2048]{1,0:T(8,128)(2,1)} %get-tuple-element.59.u_ref, f32[512,128]{1,0:T(8,128)} %get-tuple-element.60.dbc_ref, ...), custom_call_target="tpu_custom_call" | custom-call | tf_op jit(solution)/shard_map/scan_forward/pallas_call | solution.py:659
  86.7 23.4 %middle.1 = (bf16[512,1024]{1,0:T(8,128)(2,1)}, f32[512,2048]{1,0:T(8,128)}, bf16[512,2048]{1,0:T(8,128)(2,1)}, bf16[2048,1024]{1,0:T(8,128)(2,1)}, bf16[1024,20...) custom-call(bf16[512,1024]{1,0:T(8,128)(2,1)} %get-tuple-element.57.xn_ref, ...), custom_call_target="tpu_custom_call" | custom-call | tf_op jit(solution)/shard_map/middle/pallas_call | solution.py:733
  110.1 0.6 convert_element_type.22.rate_ref
  110.8 61.7 %scan_backward.1 = (f32[512,2048]{1,0:T(8,128)}, bf16[512,128]{1,0:T(8,128)(2,1)}, f32[16,2048]{1,0:T(8,128)}, f32[128,2048]{1,0:T(8,128)}, f32[1,2048]{1,0:T(1,...) custom-call(bf16[512,2048]{1,0:T(8,128)(2,1)} %get-tuple-element.59.u_ref, f32[32,16,2048]{2,1,0:T(8,128)} %bitcast.38, ...), custom_call_target="tpu_custom_call" | custom-call | tf_op jit(solution)/shard_map/scan_backward/pallas_call | solution.py:907
  172.5 1.6 mul.11.alog_ref
  174.1 75.7 %tail.1 = (f32[512,1024]{1,0:T(8,128)}, bf16[2,2,2,32,2048]{4,3,2,1,0:T(8,128)(2,1)}, bf16[2,2,2,64,1024]{4,3,2,1,0:T(8,128)(2,1)}, bf16[2,2,2,32,2048]{4,3,2,1,...) custom-call(f32[512,2048]{1,0:T(8,128)} %get-tuple-element.71.du_ref, ...), custom_call_target="tpu_custom_call" | custom-call | tf_op jit(solution)/shard_map/tail/pallas_call | solution.py:1111
  249.8 0.0 copy-start
  249.8 5.5 %finish.1 = (f32[256,4096]{1,0:T(8,128)}, f32[512,1024]{1,0:T(8,128)}, f32[64,512]{1,0:T(8,128)}, f32[16,512]{1,0:T(8,128)}, f32[512,96]{1,0:T(8,128)}, /*index=...) custom-call(bf16[256,2048]{1,0:T(8,128)(2,1)} %bitcast.48, ...), custom_call_target="tpu_custom_call" | custom-call | tf_op jit(solution)/shard_map/finish/pallas_call | solution.py:1198
  255.3 1.8 copy.30
  257.1 0.0 copy-done
  257.1 1.3 copy.35
  (1 shorter events, 0.0 us)
Async XLA Ops:
  249.8 7.3 %copy-start = (f32[512,1024]{1,0:T(8,128)S(1)}, f32[512,1024]{1,0:T(8,128)}, u32[]{:S(2)}) copy-start(f32[512,1024]{1,0:T(8,128)} %get-tuple-element.125) | copy-start | bytes 6291460

commit v3 on v2

--- a/solution.py
+++ b/solution.py
@@ -23,7 +23,7 @@
 NORM_TIME = 12
 NEVER = 1e30
 LOG2E = 1.4426950408889634
-FORWARD_STEPS = (0, 4, 7, 9, 12, 14)
+FORWARD_STEPS = (0, 4, 6, 7, 7, 9, 9, 11, 11, 13, 13, 13, 14)
 BACKWARD_TIMES = (
     ((0, 2.1, 6.1, 9.1, 11.1, 13.1), (0, 3.1, 7.1, 10.1, 12.1, 14.1)),
     ((0, 4.1, 8.1, 11.2, 13.2, 15.1), (0, 5.1, 9.2, 12.2, 14.2, 16.1)),
@@ -117,8 +117,12 @@
         self.beyond = 2 * (1 - pair) + 1 - core
         bit, low = self.own["bit"], self.own["low"]
         self.kinds = ((bit, low), (1 - bit, low), (bit, 1 - low), (1 - bit, 1 - low))
-        self.stages = [self.begin, *(functools.partial(self.from_pair, half) for half in range(2))]
-        self.stages += [*(functools.partial(self.from_near, half) for half in range(2)), self.from_far, self.end]
+        pair, near, far = (
+            [[functools.partial(stage, a, half) for half in range(2)] for a in range(2)]
+            for stage in (self.from_pair, self.from_near, self.from_far)
+        )
+        self.stages = [self.begin, pair[0][0], pair[0][1], near[0][0], pair[1][0], near[0][1], pair[1][1]]
+        self.stages += [far[0][0], far[1][0], near[1][0], far[0][1], far[1][1], near[1][1], self.end]
 
     def eighth(self, a, kind, half):
         rows = self.shards[a].shape[0] // 8
@@ -148,16 +152,17 @@
         for a in range(self.count):
             if self.in_place(a):
                 self.made()
-            for half in range(2):
-                self.link.send(functools.partial(self.to_pair, a, half))
+            for kind in (0, 3)[: a + 1]:
+                for half in range(2):
+                    self.link.send(functools.partial(self.to_pair, a, kind, half))
         for a in range(self.count):
             if not self.in_place(a):
                 self.load(a).start()
             self.link.send(functools.partial(self.own_to_core, a))
 
-    def to_pair(self, a, half):
-        rows = self.eighth(a, 0, half)
-        return self.shards[a].at[rows], self.outs[a].at[self.mine, rows], self.hop(a, 0, half), "pair"
+    def to_pair(self, a, kind, half):
+        rows = self.eighth(a, kind, half)
+        return self.shards[a].at[rows], self.outs[a].at[self.mine, rows], self.hop(a, kind, half), "pair"
 
     def own_to_core(self, a):
         return self.shards[a], self.outs[a].at[self.mine], self.whole(a), "core"
@@ -176,30 +181,25 @@
         self.link.receive(self.came(a, kind, half), self.hop(a, kind, half), dim)
         self.pass_on(a, kind, half, kind, "core")
 
-    def from_pair(self, half):
-        for a in range(self.count):
-            self.arrive(a, 0, half, "pair")
-            self.pass_on(a, 0, half, 1, "bit")
-            self.pass_on(a, 0, half, 2, "low")
+    def from_pair(self, a, half):
+        self.arrive(a, 0, half, "pair")
+        self.pass_on(a, 0, half, 1, "bit")
+        self.pass_on(a, 0, half, 2, "low")
         if half == 1:
-            for a in range(self.count):
-                if not self.in_place(a):
-                    self.load(a).wait()
-                self.store(a).start()
-
-    def from_near(self, half):
-        for a in range(self.count):
-            self.arrive(a, 1, half, "bit")
-            if half == 0:
-                self.pass_on(a, 1, 0, 3, "low")
-            self.arrive(a, 2, half, "low")
-            if half == 1:
-                self.pass_on(a, 2, 1, 3, "bit")
-
-    def from_far(self):
-        for a in range(self.count):
-            self.arrive(a, 3, 0, "low")
-            self.arrive(a, 3, 1, "bit")
+            if not self.in_place(a):
+                self.load(a).wait()
+            self.store(a).start()
+
+    def from_near(self, a, half):
+        self.arrive(a, 1, half, "bit")
+        if a == 0 and half == 0:
+            self.pass_on(a, 1, 0, 3, "low")
+        self.arrive(a, 2, half, "low")
+        if a == 0 and half == 1:
+            self.pass_on(a, 2, 1, 3, "bit")
+
+    def from_far(self, a, half):
+        self.arrive(a, 3, half, "pair" if a == 1 else ("low", "bit")[half])
 
     def end(self):
         for a in range(self.count):

time: 259 us -> 252 us (0.973)
  Pallas kernels: 243 us -> 237 us
    pallas_call x1, Pallas kernels: 39.1 us -> 32.7 us  [scan_forward(): pl.pallas_call(functools.partial(forward_kernel, rank, group, count), gri...]
where the time goes in v3:
time: 252 us
  Pallas kernels  237 us (94%)
  local copies, waits for them, and re-layouts  9.24 us (4%)
  other arithmetic  4.98 us (2%)
    pallas_call x1, Pallas kernels, tail(): pl.pallas_call(functools.partial(tail_kernel, steps, rank, count), grid=(...  75.6 us
    pallas_call x1, Pallas kernels, scan_backward(): pl.pallas_call(functools.partial(backward_kernel, rank, count, steps), gr...  62.7 us
    pallas_call x1, Pallas kernels, scan_forward(): pl.pallas_call(functools.partial(forward_kernel, rank, group, count), gri...  32.7 us
    pallas_call x1, Pallas kernels, gather_weights(): pl.pallas_call(functools.partial(gather_kernel, shapes[0][1]), out_shape=...  25.2 us
    pallas_call x1, Pallas kernels, middle(): pl.pallas_call(middle_kernel, grid=(width // block,), in_specs=[whole_spe...  23.4 us
    pallas_call x1, Pallas kernels, front(): pl.pallas_call(front_kernel, grid=(width // block,), in_specs=[pl.BlockSp...  11.6 us
    unnamed x6, local copies, waits for them, and re-layouts  6.02 us
    pallas_call x1, Pallas kernels, finish(): pl.pallas_call(functools.partial(finish_kernel, rank, states), grid=(step...  5.55 us

profile of v3, /device:TPU:0, one launch (start us, length us, event | category | flops | bytes accessed | tf_op | source)
XLA Modules:
  0.0 251.7 jit_solution(14716812481343266882)
XLA Ops:
  0.6 1.7 copy.26.xproj_ref
  2.3 25.2 %gather_weights.1 = (bf16[4,256,2048]{2,1,0:T(8,128)(2,1)}, bf16[4,256,512]{2,1,0:T(8,128)(2,1)}) custom-call(bf16[256,4096]{1,0:T(8,128)(2,1)} %refs_0_.1, bf16[64,512]{1,0:T(8,128)(2,1)} %dtproj_ref.1, bf16[16,512]{1,0:T(8,128)(2,1)} %alog_ref.1, bf16[512,96]{1,0:T(8,128)(2,1)} %copy.26.xproj_ref, bf16[4,512]{1,0:T(4,128)(2,1)} %taps_ref.1, ...), custom_call_target="tpu_custom_call" | custom-call | tf_op jit(solution)/shard_map/gather_weights/pallas_call | solution.py:262
  27.5 0.8 slice.30
  28.3 0.6 convert.2.rows_ref
  28.9 1.3 slice_bitcast_fusion
  30.2 0.9 copy.31
  31.1 0.7 slice.23
  31.8 0.6 convert.3.gain_ref
  32.4 11.6 %front.1 = (bf16[512,2048]{1,0:T(8,128)(2,1)}, f32[512,2048]{1,0:T(8,128)}, bf16[512,2048]{1,0:T(8,128)(2,1)}, f32[512,128]{1,0:T(8,128)}, bf16[512,1024]{1,0:T(...) custom-call(s32[1,8]{1,0:T(1,128)} %lens_ref.1, s32[1,8]{1,0:T(1,128)} %start_ref.1, ...), custom_call_target="tpu_custom_call" | custom-call | tf_op jit(solution)/shard_map/front/pallas_call | solution.py:538
  44.1 0.9 negate_bitcast_fusion
  45.0 0.7 broadcast_multiply_fusion.rate_ref.rate2_ref
  45.6 0.9 copy.32
  46.5 32.7 %scan_forward.1 = (f32[512,2048]{1,0:T(8,128)}, bf16[8192,2048]{1,0:T(8,128)(2,1)}, f32[512,2048]{1,0:T(8,128)}, bf16[4,256,2048]{2,1,0:T(8,128)(2,1)}, bf16[4,512,1024]{2,1,0:T(8,128)(2,1)}) custom-call(bf16[512,2048]{1,0:T(8,128)(2,1)} %get-tuple-element.59.u_ref, f32[512,128]{1,0:T(8,128)} %get-tuple-element.60.dbc_ref, ...), custom_call_target="tpu_custom_call" | custom-call | tf_op jit(solution)/shard_map/scan_forward/pallas_call | solution.py:659
  79.2 23.4 %middle.1 = (bf16[512,1024]{1,0:T(8,128)(2,1)}, f32[512,2048]{1,0:T(8,128)}, bf16[512,2048]{1,0:T(8,128)(2,1)}, bf16[2048,1024]{1,0:T(8,128)(2,1)}, bf16[1024,20...) custom-call(bf16[512,1024]{1,0:T(8,128)(2,1)} %get-tuple-element.57.xn_ref, ...), custom_call_target="tpu_custom_call" | custom-call | tf_op jit(solution)/shard_map/middle/pallas_call | solution.py:733
  102.6 0.6 convert_element_type.22.rate_ref
  103.3 62.7 %scan_backward.1 = (f32[512,2048]{1,0:T(8,128)}, bf16[512,128]{1,0:T(8,128)(2,1)}, f32[16,2048]{1,0:T(8,128)}, f32[128,2048]{1,0:T(8,128)}, f32[1,2048]{1,0:T(1,...) custom-call(bf16[512,2048]{1,0:T(8,128)(2,1)} %get-tuple-element.59.u_ref, f32[32,16,2048]{2,1,0:T(8,128)} %bitcast.38, ...), custom_call_target="tpu_custom_call" | custom-call | tf_op jit(solution)/shard_map/scan_backward/pallas_call | solution.py:907
  165.9 1.6 mul.11.alog_ref
  167.5 75.6 %tail.1 = (f32[512,1024]{1,0:T(8,128)}, bf16[2,2,2,32,2048]{4,3,2,1,0:T(8,128)(2,1)}, bf16[2,2,2,64,1024]{4,3,2,1,0:T(8,128)(2,1)}, bf16[2,2,2,32,2048]{4,3,2,1,...) custom-call(f32[512,2048]{1,0:T(8,128)} %get-tuple-element.71.du_ref, ...), custom_call_target="tpu_custom_call" | custom-call | tf_op jit(solution)/shard_map/tail/pallas_call | solution.py:1111
  243.1 0.0 copy-start
  243.1 5.5 %finish.1 = (f32[256,4096]{1,0:T(8,128)}, f32[512,1024]{1,0:T(8,128)}, f32[64,512]{1,0:T(8,128)}, f32[16,512]{1,0:T(8,128)}, f32[512,96]{1,0:T(8,128)}, /*index=...) custom-call(bf16[256,2048]{1,0:T(8,128)(2,1)} %bitcast.48, ...), custom_call_target="tpu_custom_call" | custom-call | tf_op jit(solution)/shard_map/finish/pallas_call | solution.py:1198
  248.6 1.8 copy.30
  250.4 0.0 copy-done
  250.4 1.3 copy.35
  (1 shorter events, 0.0 us)
Async XLA Ops:
  243.1 7.3 %copy-start = (f32[512,1024]{1,0:T(8,128)S(1)}, f32[512,1024]{1,0:T(8,128)}, u32[]{:S(2)}) copy-start(f32[512,1024]{1,0:T(8,128)} %get-tuple-element.125) | copy-start | bytes 6291460

commit v4 on v3

--- a/solution.py
+++ b/solution.py
@@ -987,6 +987,10 @@
     loads = [(w_ref, w_s), (tokens_ref, x_s), (cot_ref, cot_s), (dgate_ref, dxn)]
     loads = [functools.partial(pltpu.make_async_copy, src, dst, load_sem.at[i]) for i, (src, dst) in enumerate(loads)]
 
+    def store(i):
+        src, dst = (dxn, tokengrad_ref) if i == len(outs) else (spreadings[i].full, outs[i])
+        return pltpu.make_async_copy(src, dst, out_sem.at[i])
+
     def start():
         for load in loads:
             load().start()
@@ -1026,7 +1030,8 @@
         gain_grad = jnp.sum(dxn[...] * x_hat, axis=0, keepdims=True)
         d_hat = dxn[...] * gain_ref[...]
         level = jnp.mean(d_hat * x_hat, axis=1, keepdims=True)
-        tokengrad_ref[...] = cot_s[...].astype(wide) + inv * (d_hat - x_hat * level)
+        dxn[...] = cot_s[...].astype(wide) + inv * (d_hat - x_hat * level)
+        store(len(outs)).start()
         size = gain_grad.shape[1] // 4
         rows, lanes = gain_s.shape[5:]
         gain_s[...] = jnp.zeros_like(gain_s)
@@ -1035,6 +1040,10 @@
             block = jnp.concatenate(parts + [jnp.zeros((rows - len(parts), lanes), wide)], axis=0)
             gain_s[shard % 2, shard // 2, 0, 0, 0] = block.astype(low)
 
+    taken = [[times] for times in SPREAD_TIMES] + [INNER_TIMES, SMALL_TIMES, GAIN_TIMES]
+    for i, part_times in enumerate(taken):
+        last = max(times[-1] for times in part_times) + 0.001
+        events.append((last, functools.partial(lambda i: store(i).start(), i)))
     events += [(time, functools.partial(through_inner, chunk)) for chunk, time in enumerate(DXN_TIMES)]
     events.append((NORM_TIME, through_norm))
     run_events([(0, start)], final)
@@ -1085,11 +1094,8 @@
 
     @pl.when(here == final)
     def _():
-        stores = [pltpu.make_async_copy(s.full, o, out_sem.at[i]) for i, (s, o) in enumerate(zip(spreadings, outs))]
-        for copy in stores:
-            copy.start()
-        for copy in stores:
-            copy.wait()
+        for i in range(len(outs) + 1):
+            store(i).wait()
         link.finish()
 
 
@@ -1129,7 +1135,7 @@
             whole_spec(skip_grad.shape),
             *(whole_spec(p.shape) for p in pieces),
         ],
-        out_specs=[whole_spec(tokens.shape), *[pl.BlockSpec(memory_space=pl.ANY)] * (count + 3)],
+        out_specs=[pl.BlockSpec(memory_space=pl.ANY)] * (count + 4),
         out_shape=[
             jax.ShapeDtypeStruct(tokens.shape, wide),
             *(jax.ShapeDtypeStruct((2, 2, 2) + shape, low) for shape in shapes),
@@ -1146,7 +1152,7 @@
             pltpu.VMEM((2, 2, 2, 2, 2) + small_shape, low),
             pltpu.VMEM((2, 2, 2, 2, 2) + gain_shape, low),
             pltpu.SemaphoreType.DMA((4,)),
-            pltpu.SemaphoreType.DMA((count + 3,)),
+            pltpu.SemaphoreType.DMA((count + 4,)),
             *Halving.scratch(inner_shape, len(TAIL_ORDERS[2])),
             *Halving.scratch(small_shape, len(TAIL_ORDERS[3])),
             *Halving.scratch(gain_shape, len(TAIL_ORDERS[4])),

time: 252 us -> 250 us (level)
  Pallas kernels: 237 us -> 234 us
where the time goes in v4:
time: 250 us; the launch traced here: 249 us
  Pallas kernels  234 us (94%)
  local copies, waits for them, and re-layouts  9.24 us (4%)
  other arithmetic  4.98 us (2%)
    pallas_call x1, Pallas kernels, tail(): pl.pallas_call(functools.partial(tail_kernel, steps, rank, count), grid=(...  73.1 us
    pallas_call x1, Pallas kernels, scan_backward(): pl.pallas_call(functools.partial(backward_kernel, rank, count, steps), gr...  62.7 us
    pallas_call x1, Pallas kernels, scan_forward(): pl.pallas_call(functools.partial(forward_kernel, rank, group, count), gri...  32.7 us
    pallas_call x1, Pallas kernels, gather_weights(): pl.pallas_call(functools.partial(gather_kernel, shapes[0][1]), out_shape=...  25.2 us
    pallas_call x1, Pallas kernels, middle(): pl.pallas_call(middle_kernel, grid=(width // block,), in_specs=[whole_spe...  23.4 us
    pallas_call x1, Pallas kernels, front(): pl.pallas_call(front_kernel, grid=(width // block,), in_specs=[pl.BlockSp...  11.6 us
    unnamed x6, local copies, waits for them, and re-layouts  6.02 us
    pallas_call x1, Pallas kernels, finish(): pl.pallas_call(functools.partial(finish_kernel, rank, states), grid=(step...  5.55 us

profile of v4, /device:TPU:0, one launch (start us, length us, event | category | flops | bytes accessed | tf_op | source)
XLA Modules:
  0.0 249.3 jit_solution(9521546838153430614)
XLA Ops:
  0.6 1.7 copy.26.xproj_ref
  2.3 25.2 %gather_weights.1 = (bf16[4,256,2048]{2,1,0:T(8,128)(2,1)}, bf16[4,256,512]{2,1,0:T(8,128)(2,1)}) custom-call(bf16[256,4096]{1,0:T(8,128)(2,1)} %refs_0_.1, bf16[64,512]{1,0:T(8,128)(2,1)} %dtproj_ref.1, bf16[16,512]{1,0:T(8,128)(2,1)} %alog_ref.1, bf16[512,96]{1,0:T(8,128)(2,1)} %copy.26.xproj_ref, bf16[4,512]{1,0:T(4,128)(2,1)} %taps_ref.1, ...), custom_call_target="tpu_custom_call" | custom-call | tf_op jit(solution)/shard_map/gather_weights/pallas_call | solution.py:262
  27.5 0.8 slice.30
  28.3 0.6 convert.2.rows_ref
  28.9 1.3 slice_bitcast_fusion
  30.2 0.9 copy.31
  31.1 0.7 slice.23
  31.8 0.6 convert.3.gain_ref
  32.4 11.6 %front.1 = (bf16[512,2048]{1,0:T(8,128)(2,1)}, f32[512,2048]{1,0:T(8,128)}, bf16[512,2048]{1,0:T(8,128)(2,1)}, f32[512,128]{1,0:T(8,128)}, bf16[512,1024]{1,0:T(...) custom-call(s32[1,8]{1,0:T(1,128)} %lens_ref.1, s32[1,8]{1,0:T(1,128)} %start_ref.1, ...), custom_call_target="tpu_custom_call" | custom-call | tf_op jit(solution)/shard_map/front/pallas_call | solution.py:538
  44.1 0.9 negate_bitcast_fusion
  45.0 0.7 broadcast_multiply_fusion.rate_ref.rate2_ref
  45.6 0.9 copy.32
  46.5 32.7 %scan_forward.1 = (f32[512,2048]{1,0:T(8,128)}, bf16[8192,2048]{1,0:T(8,128)(2,1)}, f32[512,2048]{1,0:T(8,128)}, bf16[4,256,2048]{2,1,0:T(8,128)(2,1)}, bf16[4,512,1024]{2,1,0:T(8,128)(2,1)}) custom-call(bf16[512,2048]{1,0:T(8,128)(2,1)} %get-tuple-element.59.u_ref, f32[512,128]{1,0:T(8,128)} %get-tuple-element.60.dbc_ref, ...), custom_call_target="tpu_custom_call" | custom-call | tf_op jit(solution)/shard_map/scan_forward/pallas_call | solution.py:659
  79.2 23.4 %middle.1 = (bf16[512,1024]{1,0:T(8,128)(2,1)}, f32[512,2048]{1,0:T(8,128)}, bf16[512,2048]{1,0:T(8,128)(2,1)}, bf16[2048,1024]{1,0:T(8,128)(2,1)}, bf16[1024,20...) custom-call(bf16[512,1024]{1,0:T(8,128)(2,1)} %get-tuple-element.57.xn_ref, ...), custom_call_target="tpu_custom_call" | custom-call | tf_op jit(solution)/shard_map/middle/pallas_call | solution.py:733
  102.6 0.6 convert_element_type.22.rate_ref
  103.3 62.7 %scan_backward.1 = (f32[512,2048]{1,0:T(8,128)}, bf16[512,128]{1,0:T(8,128)(2,1)}, f32[16,2048]{1,0:T(8,128)}, f32[128,2048]{1,0:T(8,128)}, f32[1,2048]{1,0:T(1,...) custom-call(bf16[512,2048]{1,0:T(8,128)(2,1)} %get-tuple-element.59.u_ref, f32[32,16,2048]{2,1,0:T(8,128)} %bitcast.38, ...), custom_call_target="tpu_custom_call" | custom-call | tf_op jit(solution)/shard_map/scan_backward/pallas_call | solution.py:907
  165.9 1.6 mul.11.alog_ref
  167.5 73.1 %tail.1 = (f32[512,1024]{1,0:T(8,128)}, bf16[2,2,2,32,2048]{4,3,2,1,0:T(8,128)(2,1)}, bf16[2,2,2,64,1024]{4,3,2,1,0:T(8,128)(2,1)}, bf16[2,2,2,32,2048]{4,3,2,1,...) custom-call(f32[512,2048]{1,0:T(8,128)} %get-tuple-element.71.du_ref, ...), custom_call_target="tpu_custom_call" | custom-call | tf_op jit(solution)/shard_map/tail/pallas_call | solution.py:1117
  240.6 0.0 copy-start
  240.6 5.5 %finish.1 = (f32[256,4096]{1,0:T(8,128)}, f32[512,1024]{1,0:T(8,128)}, f32[64,512]{1,0:T(8,128)}, f32[16,512]{1,0:T(8,128)}, f32[512,96]{1,0:T(8,128)}, /*index=...) custom-call(bf16[256,2048]{1,0:T(8,128)(2,1)} %bitcast.48, ...), custom_call_target="tpu_custom_call" | custom-call | tf_op jit(solution)/shard_map/finish/pallas_call | solution.py:1204
  246.2 1.8 copy.30
  247.9 0.0 copy-done
  247.9 1.3 copy.35
  (1 shorter events, 0.0 us)
Async XLA Ops:
  240.6 7.3 %copy-start = (f32[512,1024]{1,0:T(8,128)S(1)}, f32[512,1024]{1,0:T(8,128)}, u32[]{:S(2)}) copy-start(f32[512,1024]{1,0:T(8,128)} %get-tuple-element.125) | copy-start | bytes 6291460
